TPU v7x, 512 devices: a whole 4x8x8 slice. The times are simulated.
512 devices in a mesh: member: 16 (over z, core), cell: 32 (over y, x).
Axes of the slice: x: 4, y: 8, z: 8, core: 2. Of those that a mesh axis runs over, the one named last changes fastest.
Arguments:
- preds: bfloat16 [16, 100, 32768], P('member', None, 'cell'), may hold values from -6 to 6
- target: bfloat16 [100, 32768], P(None, 'cell'), may hold values from -6 to 6
- area: float32 [32768], P('cell'), may hold values from 0.1 to 1
- channel_weight: float32 [100], replicated, may hold values from 0.1 to 1
- neighbours: int32 [4, 32768], P(None, 'cell'), may hold values from 0 to 32767, as said below
Outputs:
- losses: float32 [4], replicated
- grad: float32 [16, 100, 32768], P('member', None, 'cell')
Inputs may be any that keep to these rules, and one draw needn't show every extreme that they name: Each neighbour lies within 720 cells of its cell; neighbours[0] is 720 cells before and neighbours[1] 720 cells after, clipped to the grid.
All inputs are finite; a program needn't handle non-finite values.
Results may differ from a plain program's by a relative error of at most 0.0004.
Values sent between devices are 32-bit elements; how exact they have to be, the bound alone decides.
No kernel may reach another device: no remote copies, remote signals or barrier semaphores. Data moves between devices by JAX's collectives and lax.ppermute only.
A program may use at most 64 MiB of HBM per device.

v0:
```python
import jax
import jax.numpy as jnp
from jax import lax
from jax.sharding import PartitionSpec as P

ROW = 720
NEIGH = 4


ALPHA = 0.5
DELTA = 0.1


def padded(block, sides, width):
    for axis, dim in sides:
        count = lax.axis_size(axis)
        forward = [(i, i + 1) for i in range(count - 1)]
        backward = [(target, source) for source, target in forward]
        low = lax.ppermute(
            lax.slice_in_dim(block, block.shape[dim] - width, None, axis=dim), axis, forward
        )
        high = lax.ppermute(lax.slice_in_dim(block, 0, width, axis=dim), axis, backward)
        block = jnp.concatenate([low, block, high], axis=dim)
    return block


def smooth(field, flat_index):
    width = field.shape[2]
    extended = padded(field, (("cell", 2),), ROW)
    picked = jnp.take(extended, flat_index, axis=2)
    total = jnp.sum(picked.reshape(field.shape[0], field.shape[1], NEIGH, width), axis=2)
    return (1.0 - ALPHA) * field + ALPHA / NEIGH * total


def smooth_back(slope, flat_index):
    width = slope.shape[2]
    tiled = jnp.concatenate([slope] * NEIGH, axis=2)
    extended = jnp.zeros((slope.shape[0], slope.shape[1], width + 2 * ROW), jnp.float32)
    extended = extended.at[:, :, flat_index].add(tiled)
    edges_both = jnp.concatenate([extended[:, :, :ROW], extended[:, :, width + ROW :]], axis=2)
    arrived = padded(edges_both, (("cell", 2),), ROW)
    middle = extended[:, :, ROW : ROW + width]
    middle = middle.at[:, :, :ROW].add(arrived[:, :, :ROW])
    middle = middle.at[:, :, width - ROW :].add(arrived[:, :, 3 * ROW :])
    return (1.0 - ALPHA) * slope + ALPHA / NEIGH * middle


def pair_group(members):
    diff = members[:, None] - members[None, :]
    root = jnp.sqrt(diff * diff + DELTA * DELTA)
    value = jnp.sum(root - DELTA, axis=(0, 1))
    slope = jnp.sum(diff / root, axis=1)
    return (value, slope)


def crps_terms(members, truth, coef):
    count, channels, block = members.shape
    groups = 4
    split = jnp.moveaxis(members.reshape(count, groups, channels // groups, block), 1, 0)
    value, slope = lax.map(pair_group, split)
    value = value.reshape(channels, block)
    slope = jnp.moveaxis(slope, 0, 1).reshape(count, channels, block)
    direct = members - truth[None]
    root = jnp.sqrt(direct * direct + DELTA * DELTA)
    direct_sum = jnp.sum(root - DELTA, axis=0)
    loss = jnp.sum(coef * (direct_sum / count - value / (2.0 * count * (count - 1))))
    gradient = coef[None] * (direct / root / count - slope / (count * (count - 1)))
    return (loss, gradient)


def local(preds, target, area, channel_weight, neighbours):
    local_members = preds.shape[0]
    width = preds.shape[2]
    groups = lax.axis_size("member")
    block = width // groups
    first_cell = lax.axis_index("cell") * width
    flat_index = (neighbours - first_cell + ROW).reshape(NEIGH * width)
    members_raw = preds.astype(jnp.float32)
    joined = jnp.concatenate([members_raw, target.astype(jnp.float32)[None]], axis=0)
    level_one = smooth(joined, flat_index)
    level_two = smooth(level_one, flat_index)
    level_four = smooth(smooth(level_two, flat_index), flat_index)
    moved = (
        lax.all_to_all(members_raw, "member", split_axis=2, concat_axis=0, tiled=True),
        lax.all_to_all(
            level_one[:local_members], "member", split_axis=2, concat_axis=0, tiled=True
        ),
        lax.all_to_all(
            level_two[:local_members], "member", split_axis=2, concat_axis=0, tiled=True
        ),
        lax.all_to_all(
            level_four[:local_members], "member", split_axis=2, concat_axis=0, tiled=True
        ),
    )
    offset = lax.axis_index("member") * block
    area_part = lax.dynamic_slice_in_dim(area, offset, block, 0)
    coef = channel_weight[:, None] * area_part[None, :]
    numerators = []
    slopes = []
    for level, gathered in zip((joined, level_one, level_two, level_four), moved):
        truth = lax.dynamic_slice_in_dim(level[local_members], offset, block, 1)
        loss, gradient = crps_terms(gathered, truth, coef)
        numerators.append(loss)
        slopes.append(gradient)
    sums, area_total = lax.psum((jnp.stack(numerators), jnp.sum(area_part)), ("member", "cell"))
    scaling = 1.0 / (jnp.sum(channel_weight) * area_total)
    losses = sums * scaling
    returned = lax.all_to_all(
        tuple((part * scaling for part in slopes)),
        "member",
        split_axis=0,
        concat_axis=2,
        tiled=True,
    )
    inner = smooth_back(smooth_back(returned[3], flat_index), flat_index)
    inner = smooth_back(returned[2] + inner, flat_index)
    grad = returned[0] + smooth_back(returned[1] + inner, flat_index)
    return (losses, grad)


def solution(mesh):
    in_specs = (P("member", None, "cell"), P(None, "cell"), P("cell"), P(), P(None, "cell"))
    out_specs = (P(), P("member", None, "cell"))
    return jax.shard_map(local, mesh=mesh, in_specs=in_specs, out_specs=out_specs, check_vma=False)
```

profile of v0, /device:TPU:1, one launch (start us, length us, event | category | flops | bytes accessed | tf_op | source)
XLA Modules:
  0.0 809.8 jit_solution(16042477785911732273)
XLA Ops:
  3.3 11.8 %all-to-all-start = ((f32[1,100,1024]{1,0,2:T(1,128)}), f32[1,100,1024]{1,0,2:T(1,128)}, u32[]{:S(2)}, u32[]{:S(2)}) async-start(f32[1,100,1024]{1,0,2:T(1,128)} %convert_element_type.6), calls=%async_computation | async-start | bytes 1048576 | tf_op jit(solution)/shard_map/all_to_all | solution.py:84
  41.9 9.0 %pad_maximum_fusion = f32[2,100,2464]{1,0,2:T(2,128)S(1)} fusion(f32[2,100,720]{1,0,2:T(2,128)} %copy.94, f32[1,100,1024]{1,0,2:T(1,128)S(1)} %bitcast.183, f32[1,100,1024]{1,0,2:T(1,128)} %convert_element_type.6, f32[2,100,720]{1,0,2:T(2,128)} %copy.93), kind=kLoop, calls=%fused_computation.52 | loop fusion | flops 1478400 | bytes 3942400 | tf_op jit(solution)/shard_map/concatenate | solution.py:23
  50.9 28.2 %gather_fusion = f32[4096,2,100]{2,1,0:T(2,128)} fusion(f32[2,100,2464]{1,0,2:T(2,128)S(1)} %pad_maximum_fusion, s32[4096]{0:T(1024)S(1)} %fusion.70), kind=kCustom, calls=%fused_computation.clone | custom fusion | bytes 6569984 | tf_op jit(solution)/shard_map/jit(_take)/gather | solution.py:30
  79.1 16.9 %broadcast_select_fusion.3 = f32[4096,2,100]{2,1,0:T(2,128)} fusion(f32[4096,2,100]{2,1,0:T(2,128)} %gather_fusion, pred[4096]{0:T(1024)(128)(4,1)S(1)} %compare_and_fusion), kind=kLoop, calls=%fused_computation.51 | loop fusion | flops 819200 | bytes 6557696 | tf_op jit(solution)/shard_map/jit(_take)/select_n | solution.py:30
  115.7 9.1 %all-to-all-start.1 = ((f32[1,100,1024]{1,0,2:T(1,128)}), f32[1,100,1024]{1,0,2:T(1,128)}, u32[]{:S(2)}, u32[]{:S(2)}) async-start(f32[1,100,1024]{1,0,2:T(1,128)} %get-tuple-element.420), calls=%async_computation.1 | async-start | bytes 1048576 | tf_op jit(solution)/shard_map/all_to_all | solution.py:85
  128.2 18.0 %while.64 = (s32[]{:T(128)}, f32[4,25,64]{2,1,0:T(8,128)S(1)}, f32[4,16,25,64]{3,2,1,0:T(8,128)}, f32[4,16,25,64]{3,1,2,0:T(8,128)}, s32[]{:T(128)}) while((s32[]{:T(128)}, f32[4,25,64]{2,1,0:T(8,128)S(1)}, f32[4,16,25,64]{3,2,1,0:T(8,128)}, f32[4,16,25,64]{3,1,2,0:T(8,128)}, s32[]{:T(128)}) %tuple.184), condition=%wide.region_4.5_spmd, body=%wide.region_1.0_spmd.sunk | while | flops 2840002 | bytes 1121093 | solution.py:60
  157.5 9.8 %pad_maximum_fusion.1 = f32[2,100,2464]{1,0,2:T(2,128)} fusion(f32[2,100,720]{1,0,2:T(2,128)} %copy.102, f32[2,100,1024]{1,0,2:T(2,128)S(1)} %fusion.49, f32[2,100,720]{1,0,2:T(2,128)} %copy.101), kind=kLoop, calls=%fused_computation.53 | loop fusion | flops 985600 | bytes 3942400 | tf_op jit(solution)/shard_map/concatenate | solution.py:23
  167.3 29.9 %gather_fusion.1 = f32[4096,2,100]{2,1,0:T(2,128)} fusion(f32[2,100,2464]{1,0,2:T(2,128)} %pad_maximum_fusion.1, s32[4096]{0:T(1024)S(1)} %fusion.70), kind=kCustom, calls=%fused_computation.1.clone | custom fusion | bytes 6569984 | tf_op jit(solution)/shard_map/jit(_take)/gather | solution.py:30
  197.2 17.0 %broadcast_select_fusion.2 = f32[4096,2,100]{2,1,0:T(2,128)} fusion(f32[4096,2,100]{2,1,0:T(2,128)} %gather_fusion.1, pred[4096]{0:T(1024)(128)(4,1)S(1)} %compare_and_fusion), kind=kLoop, calls=%fused_computation.50 | loop fusion | flops 819200 | bytes 6557696 | tf_op jit(solution)/shard_map/jit(_take)/select_n | solution.py:30
  245.0 14.3 %while.65 = (s32[]{:T(128)}, f32[4,25,64]{2,1,0:T(8,128)S(1)}, f32[4,16,25,64]{3,2,1,0:T(8,128)}, f32[4,16,25,64]{3,1,2,0:T(8,128)S(1)}, s32[]{:T(128)}) while((s32[]{:T(128)}, f32[4,25,64]{2,1,0:T(8,128)S(1)}, f32[4,16,25,64]{3,2,1,0:T(8,128)}, f32[4,16,25,64]{3,1,2,0:T(8,128)S(1)}, s32[]{:T(128)}) %tuple.185), condition=%wide.region_11.13_spmd, body=%wide.region_8.12_spmd.sunk | while | flops 2840002 | bytes 1121093 | solution.py:60
  263.4 13.5 %pad_maximum_fusion.2 = f32[2,100,2464]{1,0,2:T(2,128)} fusion(f32[2,100,720]{1,0,2:T(2,128)S(1)} %copy.110, f32[2,100,1024]{1,0,2:T(2,128)S(1)} %multiply_add_fusion.2, f32[2,100,720]{1,0,2:T(2,128)S(1)} %copy.109), kind=kLoop, calls=%fused_computation.54 | loop fusion | flops 985600 | bytes 3942400 | tf_op jit(solution)/shard_map/concatenate | solution.py:23
  277.0 29.9 %gather_fusion.2 = f32[4096,2,100]{2,1,0:T(2,128)} fusion(f32[2,100,2464]{1,0,2:T(2,128)} %pad_maximum_fusion.2, s32[4096]{0:T(1024)S(1)} %fusion.70), kind=kCustom, calls=%fused_computation.2.clone | custom fusion | bytes 6569984 | tf_op jit(solution)/shard_map/jit(_take)/gather | solution.py:30
  306.9 17.1 %broadcast_select_fusion.1 = f32[4096,2,100]{2,1,0:T(2,128)} fusion(f32[4096,2,100]{2,1,0:T(2,128)} %gather_fusion.2, pred[4096]{0:T(1024)(128)(4,1)S(1)} %compare_and_fusion), kind=kLoop, calls=%fused_computation.49 | loop fusion | flops 819200 | bytes 6557696 | tf_op jit(solution)/shard_map/jit(_take)/select_n | solution.py:30
  361.0 11.0 %pad_maximum_fusion.3 = f32[2,100,2464]{1,0,2:T(2,128)} fusion(f32[2,100,720]{1,0,2:T(2,128)} %copy.116, f32[2,100,1024]{1,0,2:T(2,128)S(1)} %multiply_add_fusion.1, f32[2,100,720]{1,0,2:T(2,128)S(1)} %copy.115), kind=kLoop, calls=%fused_computation.55 | loop fusion | flops 985600 | bytes 3942400 | tf_op jit(solution)/shard_map/concatenate | solution.py:23
  372.0 29.9 %gather_fusion.3 = f32[4096,2,100]{2,1,0:T(2,128)} fusion(f32[2,100,2464]{1,0,2:T(2,128)} %pad_maximum_fusion.3, s32[4096]{0:T(1024)S(1)} %fusion.70), kind=kCustom, calls=%fused_computation.3.clone | custom fusion | bytes 6569984 | tf_op jit(solution)/shard_map/jit(_take)/gather | solution.py:30
  401.9 16.9 %broadcast_select_fusion = f32[4096,2,100]{2,1,0:T(2,128)} fusion(f32[4096,2,100]{2,1,0:T(2,128)} %gather_fusion.3, pred[4096]{0:T(1024)(128)(4,1)S(1)} %compare_and_fusion), kind=kLoop, calls=%fused_computation.48 | loop fusion | flops 819200 | bytes 6557696 | tf_op jit(solution)/shard_map/jit(_take)/select_n | solution.py:30
  435.2 13.9 %while.66 = (s32[]{:T(128)}, f32[4,25,64]{2,1,0:T(8,128)}, f32[4,16,25,64]{3,2,1,0:T(8,128)S(1)}, f32[4,16,25,64]{3,1,2,0:T(8,128)S(1)}, s32[]{:T(128)}) while((s32[]{:T(128)}, f32[4,25,64]{2,1,0:T(8,128)}, f32[4,16,25,64]{3,2,1,0:T(8,128)S(1)}, f32[4,16,25,64]{3,1,2,0:T(8,128)S(1)}, s32[]{:T(128)}) %tuple.182), condition=%wide.region_18.20_spmd, body=%wide.region_15.19_spmd.sunk | while | flops 2840002 | bytes 1270853 | solution.py:60
  456.1 13.9 %while.67 = (s32[]{:T(128)}, f32[4,25,64]{2,1,0:T(8,128)}, f32[4,16,25,64]{3,2,1,0:T(8,128)S(1)}, f32[4,16,25,64]{3,1,2,0:T(8,128)S(1)}, s32[]{:T(128)}) while((s32[]{:T(128)}, f32[4,25,64]{2,1,0:T(8,128)}, f32[4,16,25,64]{3,2,1,0:T(8,128)S(1)}, f32[4,16,25,64]{3,1,2,0:T(8,128)S(1)}, s32[]{:T(128)}) %tuple.183), condition=%wide.region_26.28_spmd, body=%wide.region_23.27_spmd.sunk | while | flops 2840002 | bytes 1270853 | solution.py:60
  477.8 108.1 %all-reduce = (f32[4]{0:T(128)S(1)}, f32[]{:T(128)}) all-reduce(f32[4]{0:T(128)S(1)} %pad_maximum_fusion.5, f32[]{:T(128)} %get-tuple-element.409), channel_id=1, replica_groups=mesh['member'=16,'cell'=32] {'member','cell'}, use_global_device_ids=true, to_apply=%region_28.30 | all-reduce | flops 5 | bytes 40 | tf_op jit(solution)/shard_map/psum | solution.py:105
  596.9 17.2 %all-to-all-done.7 = f32[16,100,64]{1,2,0:T(8,128)S(1)} async-done(((f32[16,100,64]{1,2,0:T(8,128)}), f32[16,100,64]{1,2,0:T(8,128)S(1)}, u32[]{:S(2)}, u32[]{:S(2)}) %all-to-all-start.7) | async-done | bytes 409632 | tf_op jit(solution)/shard_map/all_to_all | solution.py:108
  614.1 26.5 %scatter_custom_fusion = f32[100,2464]{0,1:T(8,128)S(1)} fusion(s32[4096]{0:T(1024)S(1)} %bitcast.224, f32[1,100,1024]{1,2,0:T(8,128)S(1)} %bitcast.204, f32[]{:T(128)} %constant.383, f32[]{:T(128)} %constant.371.clone.1), kind=kCustom, calls=%fused_computation.57 | custom fusion | flops 1638400 | bytes 1509896 | tf_op jit(solution)/shard_map/scatter-add | solution.py:39
  653.6 26.5 %scatter_custom_fusion.1 = f32[100,2464]{0,1:T(8,128)S(1)} fusion(s32[4096]{0:T(1024)S(1)} %bitcast.225, f32[1,100,1024]{1,2,0:T(8,128)S(1)} %multiply_add_fusion.3, f32[]{:T(128)} %constant.383, f32[]{:T(128)} %constant.371.clone.1), kind=kCustom, calls=%fused_computation.65 | custom fusion | flops 1638400 | bytes 1509896 | tf_op jit(solution)/shard_map/scatter-add | solution.py:39
  704.3 26.5 %scatter_custom_fusion.2 = f32[100,2464]{0,1:T(8,128)S(1)} fusion(s32[4096]{0:T(1024)S(1)} %bitcast.226, f32[1,100,1024]{1,2,0:T(8,128)S(1)} %bitcast_add_fusion, f32[]{:T(128)} %constant.383, f32[]{:T(128)} %constant.371.clone.1), kind=kCustom, calls=%fused_computation.73 | custom fusion | flops 1638400 | bytes 1509896 | tf_op jit(solution)/shard_map/scatter-add | solution.py:39
  758.0 26.5 %scatter_custom_fusion.3 = f32[100,2464]{0,1:T(8,128)S(1)} fusion(s32[4096]{0:T(1024)S(1)} %bitcast.227, f32[1,100,1024]{1,2,0:T(8,128)S(1)} %bitcast_add_fusion.1, f32[]{:T(128)} %constant.383, f32[]{:T(128)} %constant.371.clone.1), kind=kCustom, calls=%fused_computation.81 | custom fusion | flops 1638400 | bytes 1509896 | tf_op jit(solution)/shard_map/scatter-add | solution.py:39
  (265 shorter events, 325.0 us)
Async XLA Ops:
  3.3 112.4 %all-to-all-start = ((f32[1,100,1024]{1,0,2:T(1,128)}), f32[1,100,1024]{1,0,2:T(1,128)}, u32[]{:S(2)}, u32[]{:S(2)}) async-start(f32[1,100,1024]{1,0,2:T(1,128)} %convert_element_type.6), calls=%async_computation | async-start | bytes 1048576 | tf_op jit(solution)/shard_map/all_to_all | solution.py:84
  18.9 16.2 %collective-permute-start = (f32[2,100,720]{2,0,1:T(2,128)S(1)}, f32[2,100,720]{2,0,1:T(2,128)S(1)}, u32[]{:S(2)}, u32[]{:S(2)}) collective-permute-start(f32[2,100,720]{2,0,1:T(2,128)S(1)} %copy.91), channel_id=1, source_target_pairs={{0,1},{1,2},{2,3},{3,4},{4,5},{5,6},{6,7},{7,8},{8,9},{9,10},{10,1... | collective-permute-start | bytes 1728008 | tf_op jit(solution)/shard_map/ppermute | solution.py:19
  23.6 17.1 %collective-permute-start.1 = (f32[2,100,720]{2,0,1:T(2,128)}, f32[2,100,720]{2,0,1:T(2,128)S(1)}, u32[]{:S(2)}, u32[]{:S(2)}) collective-permute-start(f32[2,100,720]{2,0,1:T(2,128)} %copy.92), channel_id=1, source_target_pairs={{1,0},{2,1},{3,2},{4,3},{5,4},{6,5},{7,6},{8,7},{9,8},{10,9},{11,1... | collective-permute-start | bytes 1728008 | tf_op jit(solution)/shard_map/ppermute | solution.py:22
  106.7 46.6 %collective-permute-start.2 = (f32[2,100,720]{2,0,1:T(2,128)}, f32[2,100,720]{2,0,1:T(2,128)}, u32[]{:S(2)}, u32[]{:S(2)}) collective-permute-start(f32[2,100,720]{2,0,1:T(2,128)} %copy.99), channel_id=1, source_target_pairs={{0,1},{1,2},{2,3},{3,4},{4,5},{5,6},{6,7},{7,8},{8,9},{9,10},{10,1... | collective-permute-start | bytes 1728008 | tf_op jit(solution)/shard_map/ppermute | solution.py:19
  112.8 42.6 %collective-permute-start.3 = (f32[2,100,720]{2,0,1:T(2,128)}, f32[2,100,720]{2,0,1:T(2,128)}, u32[]{:S(2)}, u32[]{:S(2)}) collective-permute-start(f32[2,100,720]{2,0,1:T(2,128)} %copy.100), channel_id=1, source_target_pairs={{1,0},{2,1},{3,2},{4,3},{5,4},{6,5},{7,6},{8,7},{9,8},{10,9},{11,1... | collective-permute-start | bytes 1728008 | tf_op jit(solution)/shard_map/ppermute | solution.py:22
  115.7 119.0 %all-to-all-start.1 = ((f32[1,100,1024]{1,0,2:T(1,128)}), f32[1,100,1024]{1,0,2:T(1,128)}, u32[]{:S(2)}, u32[]{:S(2)}) async-start(f32[1,100,1024]{1,0,2:T(1,128)} %get-tuple-element.420), calls=%async_computation.1 | async-start | bytes 1048576 | tf_op jit(solution)/shard_map/all_to_all | solution.py:85
  224.9 35.0 %collective-permute-start.4 = (f32[2,100,720]{2,0,1:T(2,128)}, f32[2,100,720]{2,0,1:T(2,128)}, u32[]{:S(2)}, u32[]{:S(2)}) collective-permute-start(f32[2,100,720]{2,0,1:T(2,128)} %copy.107), channel_id=1, source_target_pairs={{0,1},{1,2},{2,3},{3,4},{4,5},{5,6},{6,7},{7,8},{8,9},{9,10},{10,1... | collective-permute-start | bytes 1728008 | tf_op jit(solution)/shard_map/ppermute | solution.py:19
  231.6 30.1 %collective-permute-start.5 = (f32[2,100,720]{2,0,1:T(2,128)}, f32[2,100,720]{2,0,1:T(2,128)}, u32[]{:S(2)}, u32[]{:S(2)}) collective-permute-start(f32[2,100,720]{2,0,1:T(2,128)} %copy.108), channel_id=1, source_target_pairs={{1,0},{2,1},{3,2},{4,3},{5,4},{6,5},{7,6},{8,7},{9,8},{10,9},{11,1... | collective-permute-start | bytes 1728008 | tf_op jit(solution)/shard_map/ppermute | solution.py:22
  234.6 112.1 %all-to-all-start.2 = ((f32[1,100,1024]{1,0,2:T(1,128)}), f32[1,100,1024]{1,0,2:T(1,128)S(1)}, u32[]{:S(2)}, u32[]{:S(2)}) async-start(f32[1,100,1024]{1,0,2:T(1,128)} %get-tuple-element.422), calls=%async_computation.2 | async-start | bytes 1048576 | tf_op jit(solution)/shard_map/all_to_all | solution.py:88
  334.9 17.9 %collective-permute-start.6 = (f32[2,100,720]{2,0,1:T(2,128)}, f32[2,100,720]{2,0,1:T(2,128)}, u32[]{:S(2)}, u32[]{:S(2)}) collective-permute-start(f32[2,100,720]{2,0,1:T(2,128)} %copy.113), channel_id=1, source_target_pairs={{0,1},{1,2},{2,3},{3,4},{4,5},{5,6},{6,7},{7,8},{8,9},{9,10},{10,1... | collective-permute-start | bytes 1728008 | tf_op jit(solution)/shard_map/ppermute | solution.py:19
  341.6 17.4 %collective-permute-start.7 = (f32[2,100,720]{2,0,1:T(2,128)}, f32[2,100,720]{2,0,1:T(2,128)}, u32[]{:S(2)}, u32[]{:S(2)}) collective-permute-start(f32[2,100,720]{2,0,1:T(2,128)} %copy.114), channel_id=1, source_target_pairs={{1,0},{2,1},{3,2},{4,3},{5,4},{6,5},{7,6},{8,7},{9,8},{10,9},{11,1... | collective-permute-start | bytes 1728008 | tf_op jit(solution)/shard_map/ppermute | solution.py:22
  426.2 28.7 %all-to-all-start.3 = ((f32[1,100,1024]{1,0,2:T(1,128)}), f32[1,100,1024]{1,0,2:T(1,128)S(1)}, u32[]{:S(2)}, u32[]{:S(2)}) async-start(f32[1,100,1024]{1,0,2:T(1,128)} %get-tuple-element.424), calls=%async_computation.3 | async-start | bytes 1048576 | tf_op jit(solution)/shard_map/all_to_all | solution.py:91
  591.0 23.1 %all-to-all-start.7 = ((f32[16,100,64]{1,2,0:T(8,128)}), f32[16,100,64]{1,2,0:T(8,128)S(1)}, u32[]{:S(2)}, u32[]{:S(2)}) async-start(f32[16,100,64]{1,2,0:T(8,128)} %get-tuple-element.433), calls=%async_computation.7 | async-start | bytes 1048576 | tf_op jit(solution)/shard_map/all_to_all | solution.py:108
  640.7 8.7 %collective-permute-start.8 = (f32[1,100,720]{1,2,0:T(8,128)S(1)}, f32[1,100,720]{1,2,0:T(8,128)S(1)}, u32[]{:S(2)}, u32[]{:S(2)}) collective-permute-start(f32[1,100,720]{1,2,0:T(8,128)S(1)} %get-tuple-element.418), channel_id=1, source_target_pairs={{0,1},{1,2},{2,3},{3,4},{4,5},{5,6},{6,7},{7,8},{8,9},{9,10},{10,1... | collective-permute-start | bytes 864008 | tf_op jit(solution)/shard_map/ppermute | solution.py:19
  642.0 11.5 %collective-permute-start.9 = (f32[1,100,720]{1,2,0:T(8,128)S(1)}, f32[1,100,720]{1,2,0:T(8,128)S(1)}, u32[]{:S(2)}, u32[]{:S(2)}) collective-permute-start(f32[1,100,720]{1,2,0:T(8,128)S(1)} %get-tuple-element.417), channel_id=1, source_target_pairs={{1,0},{2,1},{3,2},{4,3},{5,4},{6,5},{7,6},{8,7},{9,8},{10,9},{11,1... | collective-permute-start | bytes 864008 | tf_op jit(solution)/shard_map/ppermute | solution.py:22
  681.0 9.7 %collective-permute-start.10 = (f32[1,100,720]{1,2,0:T(8,128)}, f32[1,100,720]{1,2,0:T(8,128)}, u32[]{:S(2)}, u32[]{:S(2)}) collective-permute-start(f32[1,100,720]{1,2,0:T(8,128)} %get-tuple-element.416), channel_id=1, source_target_pairs={{0,1},{1,2},{2,3},{3,4},{4,5},{5,6},{6,7},{7,8},{8,9},{9,10},{10,1... | collective-permute-start | bytes 864008 | tf_op jit(solution)/shard_map/ppermute | solution.py:19
  683.0 21.3 %all-to-all-start.6 = ((f32[16,100,64]{1,2,0:T(8,128)}), f32[16,100,64]{1,2,0:T(8,128)S(1)}, u32[]{:S(2)}, u32[]{:S(2)}) async-start(f32[16,100,64]{1,2,0:T(8,128)} %get-tuple-element.435), calls=%async_computation.6 | async-start | bytes 1048576 | tf_op jit(solution)/shard_map/all_to_all | solution.py:108
  686.9 13.1 %collective-permute-start.11 = (f32[1,100,720]{1,2,0:T(8,128)S(1)}, f32[1,100,720]{1,2,0:T(8,128)S(1)}, u32[]{:S(2)}, u32[]{:S(2)}) collective-permute-start(f32[1,100,720]{1,2,0:T(8,128)S(1)} %get-tuple-element.415), channel_id=1, source_target_pairs={{1,0},{2,1},{3,2},{4,3},{5,4},{6,5},{7,6},{8,7},{9,8},{10,9},{11,1... | collective-permute-start | bytes 864008 | tf_op jit(solution)/shard_map/ppermute | solution.py:22
  731.7 11.2 %collective-permute-start.12 = (f32[1,100,720]{1,2,0:T(8,128)}, f32[1,100,720]{1,2,0:T(8,128)}, u32[]{:S(2)}, u32[]{:S(2)}) collective-permute-start(f32[1,100,720]{1,2,0:T(8,128)} %get-tuple-element.414), channel_id=1, source_target_pairs={{0,1},{1,2},{2,3},{3,4},{4,5},{5,6},{6,7},{7,8},{8,9},{9,10},{10,1... | collective-permute-start | bytes 864008 | tf_op jit(solution)/shard_map/ppermute | solution.py:19
  735.6 22.3 %all-to-all-start.5 = ((f32[16,100,64]{1,2,0:T(8,128)}), f32[16,100,64]{1,2,0:T(8,128)S(1)}, u32[]{:S(2)}, u32[]{:S(2)}) async-start(f32[16,100,64]{1,2,0:T(8,128)} %get-tuple-element.434), calls=%async_computation.5 | async-start | bytes 1048576 | tf_op jit(solution)/shard_map/all_to_all | solution.py:108
  740.6 12.0 %collective-permute-start.13 = (f32[1,100,720]{1,2,0:T(8,128)S(1)}, f32[1,100,720]{1,2,0:T(8,128)S(1)}, u32[]{:S(2)}, u32[]{:S(2)}) collective-permute-start(f32[1,100,720]{1,2,0:T(8,128)S(1)} %get-tuple-element.413), channel_id=1, source_target_pairs={{1,0},{2,1},{3,2},{4,3},{5,4},{6,5},{7,6},{8,7},{9,8},{10,9},{11,1... | collective-permute-start | bytes 864008 | tf_op jit(solution)/shard_map/ppermute | solution.py:22
  785.3 10.0 %collective-permute-start.14 = (f32[1,100,720]{1,2,0:T(8,128)}, f32[1,100,720]{1,2,0:T(8,128)}, u32[]{:S(2)}, u32[]{:S(2)}) collective-permute-start(f32[1,100,720]{1,2,0:T(8,128)} %get-tuple-element.412), channel_id=1, source_target_pairs={{0,1},{1,2},{2,3},{3,4},{4,5},{5,6},{6,7},{7,8},{8,9},{9,10},{10,1... | collective-permute-start | bytes 864008 | tf_op jit(solution)/shard_map/ppermute | solution.py:19
  787.9 20.5 %all-to-all-start.4 = ((f32[16,100,64]{1,2,0:T(8,128)}), f32[16,100,64]{1,2,0:T(8,128)S(1)}, u32[]{:S(2)}, u32[]{:S(2)}) async-start(f32[16,100,64]{1,2,0:T(8,128)} %get-tuple-element.436), calls=%async_computation.4 | async-start | bytes 1048576 | tf_op jit(solution)/shard_map/all_to_all | solution.py:108
  791.4 12.2 %collective-permute-start.15 = (f32[1,100,720]{1,2,0:T(8,128)S(1)}, f32[1,100,720]{1,2,0:T(8,128)S(1)}, u32[]{:S(2)}, u32[]{:S(2)}) collective-permute-start(f32[1,100,720]{1,2,0:T(8,128)S(1)} %get-tuple-element.411), channel_id=1, source_target_pairs={{1,0},{2,1},{3,2},{4,3},{5,4},{6,5},{7,6},{8,7},{9,8},{10,9},{11,1... | collective-permute-start | bytes 864008 | tf_op jit(solution)/shard_map/ppermute | solution.py:22
  (14 other events, 213.3 us)
where the time goes:
time: 818 us; the launch traced here: 810 us
  other arithmetic  317 us (39%)
  local copies, waits for them, and re-layouts  197 us (24%)
  blocking collectives  108 us (13%)
  starting transfers between devices  92.9 us (11%)
  waiting for transfers between devices  91.1 us (11%)
    gather x4, local copies, waits for them, and re-layouts, smooth(): picked = jnp.take(extended, flat_index, axis=2)  118 us
    psum x1, blocking collectives, local(): lax.psum((jnp.stack(numerators), jnp.sum(area_part)), ('member', 'cell'))  108 us
    scatter-add x4, other arithmetic, smooth_back(): extended = extended.at[:, :, flat_index].add(tiled)  106 us
    select_n x4, other arithmetic, smooth(): picked = jnp.take(extended, flat_index, axis=2)  68 us
    reduce_sum x16, other arithmetic, pair_group(): slope = jnp.sum(diff / root, axis=1)  43.8 us
    concatenate x4, other arithmetic, padded(): block = jnp.concatenate([low, block, high], axis=dim)  43.3 us
    ppermute x8, waiting for transfers between devices, padded(): lax.ppermute(lax.slice_in_dim(block, 0, width, axis=dim), axis, backward)  36.7 us
    all_to_all x4, waiting for transfers between devices, local(): lax.all_to_all(tuple((part * scaling for part in slopes)), 'member', spli...  31.2 us
  transfers between devices with their start and end apart: 24, of which 16 were waited for; matrix products, arithmetic and copies ran while one was open for 38% of the time, Pallas kernels for 0%

commit v1 on v0

v1 whole, which is shorter than its diff:
```python
import functools

import jax
import jax.numpy as jnp
from jax import lax
from jax.experimental import pallas as pl
from jax.experimental.pallas import tpu as pltpu
from jax.sharding import PartitionSpec as P

GROUP = 4
CH = 2
M = 16
LANE = 128
NEIGH = 4
ROW = 720
BLOCK = 1024
PER = BLOCK // LANE
WIDTH = GROUP * BLOCK
CHUNKS = WIDTH // LANE
TILE = 256
REACH = 3
BAND = (2 * REACH + 1) * TILE
SIDE = 4 * REACH
OWN = WIDTH // TILE
EXT = (OWN + 2 * SIDE) * TILE
BLOCKS = OWN + 2 * SIDE - 2 * REACH
EDGE = 2 * SIDE - 1
RF = 40
HIGH = 48
RB = CH * M
RT = RB + CH
WIRE = -(-(EDGE * RT + RF - RT) // 8) * 8
AUX = (CH + NEIGH + 1) * PER
AREA_AT = (CH + NEIGH) * PER
NOTE = CH * PER + 1
DELTA = 0.1
F32 = jnp.float32
BF16 = jnp.bfloat16
SMEM_SPEC = pl.BlockSpec(memory_space=pltpu.SMEM)
VMEM_SPEC = pl.BlockSpec(memory_space=pltpu.VMEM)


def shape(*dims, dtype=F32):
    return jax.ShapeDtypeStruct(dims, dtype)


def call(body, name, outs, scratch=(), scalars=0, vectors=1, limit=24):
    return pl.pallas_call(
        body,
        in_specs=[SMEM_SPEC] * scalars + [VMEM_SPEC] * vectors,
        out_specs=[VMEM_SPEC] * len(outs),
        out_shape=outs,
        scratch_shapes=list(scratch),
        compiler_params=pltpu.CompilerParams(vmem_limit_bytes=limit * 1024 * 1024),
        name=name,
    )


def pack_body(preds_ref, send_ref):
    used = preds_ref.shape[1] // CH
    size = CH * PER
    send_ref[used * size :, :] = jnp.zeros((send_ref.shape[0] - used * size, LANE), F32)
    for c in range(CH):
        for l in range(PER):
            part = preds_ref[0, c * used : (c + 1) * used, l * LANE : (l + 1) * LANE].astype(F32)
            send_ref[pl.ds(c * PER + l, used, stride=size), :] = part


def shift_of(x, mine):
    return (mine - x + GROUP) % GROUP


def unpack_body(place_ref, recv_ref, side_ref, own_ref, left_ref, right_ref, rows, tight):
    rows[...] = jnp.zeros_like(rows)
    tight[...] = jnp.zeros_like(tight)
    for x in range(GROUP):
        for r in range(RT):
            if r < RB:
                c, m = divmod(r, M)
                value = recv_ref[m * GROUP + x, c * PER : (c + 1) * PER, :]
            else:
                c = r - RB
                value = side_ref[shift_of(x, place_ref[1]), c * PER : (c + 1) * PER, :]
            rows[pl.ds(x * PER * RF + r, PER, stride=RF), :] = value
            tight[pl.ds(x * PER * RT + r, PER, stride=RT), :] = value
    for i in range(CHUNKS):
        own_ref[i] = rows[i * RF : (i + 1) * RF, :]
    left_ref[...] = tight[:WIRE, :]
    start = (CHUNKS - EDGE) * RT
    right_ref[...] = tight[start : start + WIRE, :]


def parts(value):
    high = value.astype(BF16).astype(F32)
    return jnp.concatenate([high, value - high], axis=0).astype(BF16)


def tile_at(index, count=1):
    return pl.ds(pl.multiple_of(index * TILE, TILE), count * TILE)


def builder(row_group, mine, aux_ref, band, cells):
    down = lax.broadcasted_iota(jnp.int32, (TILE, TILE), 0)
    across = lax.broadcasted_iota(jnp.int32, (TILE, TILE), 1)
    unit = jnp.where(down == across, 0.5, 0.0).astype(BF16)
    count = down.astype(F32).astype(BF16)
    weight = jnp.full((TILE, TILE), 0.5 / NEIGH, BF16)
    none = jnp.zeros((TILE, TILE), BF16)
    first_cell = row_group * WIDTH - SIDE * TILE

    def hits(relative, t):
        at = relative - float(t * TILE)
        at = jnp.where((at < 0.0) | (at > TILE - 1.0), -1.0, at).astype(BF16)
        return jnp.where(count == at, weight, none)

    def places(b, k):
        halves = []
        for h in range(2):
            chunk = CHUNKS - 2 * SIDE + 2 * (b + REACH) + h
            x = (chunk % CHUNKS) // PER
            piece = (chunk // CHUNKS) * GROUP + shift_of(x, mine)
            halves.append(aux_ref[piece, pl.ds((CH + k) * PER + chunk % PER, 1), :])
        return jnp.concatenate(halves, axis=1) - (first_cell + b * TILE).astype(F32)

    def plain(b, h, stage):
        relative = [places(b, k) for k in range(NEIGH)]
        for t in range(2 * REACH + 1):
            total = hits(relative[2], t) + hits(relative[3], t)
            if t < 2:
                total = total + hits(relative[0], t)
            if t > 2 * REACH - 2:
                total = total + hits(relative[1], t)
            if t == REACH:
                total = total + unit
            span = slice(t * TILE, (t + 1) * TILE)
            stage[h, span, :] = total
            band[b, span, :] = total

    def clipped(b, h, stage):
        cell = first_cell + (b + REACH) * TILE

        def more(k, tiles):
            relative = places(b, k)
            for t in tiles:
                span = slice(t * TILE, (t + 1) * TILE)
                total = band[b, span, :] + hits(relative, t)
                stage[h, span, :] = total
                band[b, span, :] = total

        @pl.when(cell < ROW)
        def _():
            more(0, range(2, 2 * REACH + 1))

        @pl.when(cell + TILE > cells - ROW)
        def _():
            more(1, range(2 * REACH - 1))

    return plain, clipped


def scorer(weight_ref, mine, aux_ref, rows, slopes, sums):
    square = DELTA * DELTA
    sums[...] = jnp.zeros_like(sums)

    def one(level, index):
        c = index // GROUP
        x = index % GROUP
        base = level * (2 * BLOCKS * RF) + (2 * (SIDE - REACH) + x * PER) * RF
        fields = [rows[pl.ds(base + c * M + m, PER, stride=RF), :] for m in range(M)]
        truth = rows[pl.ds(base + RB + c, PER, stride=RF), :]
        coef = aux_ref[GROUP + shift_of(x, mine), AREA_AT:, :] * weight_ref[c]
        slope = [None] * M
        inverse = jnp.zeros((PER, LANE), F32)
        for a in range(M):
            for b in range(a + 1, M):
                diff = fields[a] - fields[b]
                r = lax.rsqrt(diff * diff + square)
                s = diff * r
                inverse = inverse + r
                slope[a] = s if slope[a] is None else slope[a] + s
                slope[b] = -s if slope[b] is None else slope[b] - s
        pair = square * inverse
        direct_sum = jnp.zeros((PER, LANE), F32)
        out = (level * CHUNKS + x * PER) * RB + c * M
        for m in range(M):
            direct = fields[m] - truth
            q = direct * direct + square
            r = lax.rsqrt(q)
            direct_sum = direct_sum + q * r
            pair = pair + direct * slope[m]
            slopes[pl.ds(out + m, PER, stride=RB), :] = coef * (
                direct * r * (1.0 / M) - slope[m] * (1.0 / (M * (M - 1)))
            )
        term = direct_sum * (1.0 / M) - pair * (1.0 / (M * (M - 1))) - 0.5 * DELTA
        span = slice(level * PER, (level + 1) * PER)
        sums[span, :] = sums[span, :] + coef * term

    return one


def main_body(
    cells, place_ref, weight_ref, own_ref, left_ref, right_ref, aux_ref,
    center_ref, outl_ref, outr_ref, loss_ref, band, xs, rows, slopes, total, sums, stage_a, stage_b,
):
    row_group = place_ref[0]
    mine = place_ref[1]
    plain, clipped = builder(row_group, mine, aux_ref, band, cells)
    score = scorer(weight_ref, mine, aux_ref, rows, slopes, sums)

    xs[0, :, :LANE] = jnp.zeros((2 * RF, LANE), BF16)
    xs[0, :, EXT - LANE :] = jnp.zeros((2 * RF, LANE), BF16)
    for i in range(EDGE):
        near = slice(i * RT, i * RT + RF)
        xs[0, :, (1 + i) * LANE : (2 + i) * LANE] = parts(left_ref[near, :])
        far = 2 * (SIDE + OWN) + i
        xs[0, :, far * LANE : (far + 1) * LANE] = parts(right_ref[near, :])
    for i in range(CHUNKS):
        value = own_ref[i]
        at = 2 * SIDE + i
        xs[0, :, at * LANE : (at + 1) * LANE] = parts(value)
        at = 2 * (SIDE - REACH) + i
        rows[at * RF : (at + 1) * RF, :] = value

    def products(step, p, read):
        got = []
        for h in range(2):
            b = 2 * p + h + step * REACH
            used = HIGH if step == 0 else 2 * RF
            field = xs[step % 2, :used, tile_at(b, 2 * REACH + 1)]
            got.append(jnp.dot(field, read(b, h), preferred_element_type=F32))
        return got

    def keep(step, p, got):
        kept = {0: 1, 1: 2, 3: 3}.get(step)
        for h in range(2):
            b = 2 * p + h + step * REACH
            value = got[h][:RF]
            if step > 0:
                value = value + got[h][RF:]
            if step < 3:
                xs[(step + 1) % 2, :, tile_at(b + REACH)] = parts(value)
            if kept is not None:
                start = pl.multiple_of(kept * (2 * BLOCKS * RF) + b * (2 * RF), RF)
                rows[pl.ds(start, RF), :] = value[:, :LANE]
                rows[pl.ds(start + RF, RF), :] = value[:, LANE:]

    def build_pair(p, stage):
        for h in range(2):
            plain(2 * p + h, h, stage)

    def fix_pair(p, stage):
        for h in range(2):
            clipped(2 * p + h, h, stage)

    def use_and_build(p, stage, following):
        got = products(0, p, lambda b, h: stage[h])
        build_pair(p + 1, following)
        keep(0, p, got)
        fix_pair(p + 1, following)

    build_pair(0, stage_a)
    fix_pair(0, stage_a)

    def two_pairs(i, carry):
        use_and_build(2 * i, stage_a, stage_b)
        use_and_build(2 * i + 1, stage_b, stage_a)
        return carry

    last = BLOCKS // 2 - 1
    lax.fori_loop(0, last // 2, two_pairs, 0)
    keep(0, last, products(0, last, lambda b, h: stage_a[h]))

    for step in range(1, 4):

        def forward(scored, p, carry):
            got = products(step, p, lambda b, h: band[b])
            if scored:
                score(step - 1, p)
            keep(step, p, got)
            return carry

        split = CH * GROUP
        lax.fori_loop(0, split, functools.partial(forward, True), 0)
        lax.fori_loop(split, BLOCKS // 2 - REACH * step, functools.partial(forward, False), 0)

    def only_score(index, carry):
        score(3, index)
        return carry

    lax.fori_loop(0, CH * GROUP, only_score, 0)
    partial = [jnp.sum(sums[level * PER : (level + 1) * PER, :], axis=0, keepdims=True) for level in range(4)]
    partial.append(jnp.sum(aux_ref[GROUP, AREA_AT:, :], axis=0, keepdims=True) * (1.0 / M))
    partial.append(jnp.zeros((PER - len(partial), LANE), F32))
    partial = jnp.concatenate(partial, axis=0)
    for i in range(loss_ref.shape[0]):
        loss_ref[i] = partial

    gs = xs.at[0]
    for step in range(4):
        first = (3 - step) * REACH
        level = {0: 3, 2: 2, 3: 1}.get(step)
        if step > 0 and level is not None:
            for i in range(CHUNKS):
                at = slice((2 * SIDE + i) * LANE, (2 * SIDE + i + 1) * LANE)
                begin = (level * CHUNKS + i) * RB
                total[:, at] = total[:, at] + slopes[begin : begin + RB, :]
        if step == 0:
            for i in range(CHUNKS):
                at = slice((2 * SIDE + i) * LANE, (2 * SIDE + i + 1) * LANE)
                begin = (level * CHUNKS + i) * RB
                gs[: 2 * RB, at] = parts(slopes[begin : begin + RB, :])
        else:

            def refill(p, carry):
                at = tile_at(p + first + REACH)
                gs[: 2 * RB, at] = parts(total[:, at])
                return carry

            lax.fori_loop(0, BLOCKS - 2 * first, refill, 0)
        total[...] = jnp.zeros_like(total)

        def backward(p, carry):
            got = []
            for h in range(2):
                b = 2 * p + h + first
                got.append(
                    lax.dot_general(
                        gs[: 2 * RB, tile_at(b + REACH)],
                        band[b],
                        (((1,), (1,)), ((), ())),
                        preferred_element_type=F32,
                    )
                )
            for h in range(2):
                at = tile_at(2 * p + h + first, 2 * REACH + 1)
                total[:, at] = total[:, at] + (got[h][:RB] + got[h][RB:])
            return carry

        lax.fori_loop(0, (BLOCKS - 2 * first) // 2, backward, 0)

    for i in range(CHUNKS):
        at = 2 * SIDE + i
        center_ref[i] = total[:, at * LANE : (at + 1) * LANE] + slopes[i * RB : (i + 1) * RB, :]
    for i in range(EDGE):
        outl_ref[i] = total[:, (1 + i) * LANE : (2 + i) * LANE]
        far = 2 * (SIDE + OWN) + i
        outr_ref[i] = total[:, far * LANE : (far + 1) * LANE]


def final_body(center_ref, arrl_ref, arrr_ref, sums_ref, send_ref, rows):
    for i in range(CHUNKS):
        value = center_ref[i]
        if i < EDGE:
            value = value + arrl_ref[i]
        if i >= CHUNKS - EDGE:
            value = value + arrr_ref[i - (CHUNKS - EDGE)]
        rows[i * RB : (i + 1) * RB, :] = value
    for x in range(GROUP):
        for c in range(CH):
            for m in range(M):
                start = (m * GROUP + x) * NOTE + c * PER
                send_ref[start : start + PER, :] = rows[pl.ds(x * PER * RB + c * M + m, PER, stride=RB), :]
    sums = sums_ref[0]
    for i in range(1, sums_ref.shape[0]):
        sums = sums + sums_ref[i]
    sums = jnp.sum(sums, axis=1, keepdims=True)
    down = lax.broadcasted_iota(jnp.int32, (PER, LANE), 0)
    across = lax.broadcasted_iota(jnp.int32, (PER, LANE), 1)
    note = jnp.sum(jnp.where(down == across, sums, 0.0), axis=0, keepdims=True)
    slots = send_ref.shape[0] // NOTE
    send_ref[pl.ds(NOTE - 1, slots, stride=NOTE), :] = jnp.broadcast_to(note, (slots, LANE))


def spread_body(recv_ref, weight_ref, losses_ref, out_ref):
    slots = recv_ref.shape[0] // NOTE
    sums = jnp.sum(recv_ref[pl.ds(NOTE - 1, slots, stride=NOTE), :], axis=0, keepdims=True)
    lane = lax.broadcasted_iota(jnp.int32, (1, LANE), 1)
    area = jnp.sum(jnp.where(lane == 4, sums, 0.0), axis=1, keepdims=True)
    scale = 1.0 / (jnp.sum(weight_ref[...], axis=1, keepdims=True) * area)
    losses_ref[...] = jnp.broadcast_to(sums * scale, losses_ref.shape)
    used = out_ref.shape[1] // CH
    for c in range(CH):
        for l in range(PER):
            part = recv_ref[pl.ds(c * PER + l, used, stride=NOTE), :]
            out_ref[0, c * used : (c + 1) * used, l * LANE : (l + 1) * LANE] = part * scale


def local(preds, target, area, channel_weight, neighbours):
    members = lax.axis_size("member")
    cells = lax.axis_size("cell")
    channels = preds.shape[1]
    member = lax.axis_index("member")
    cell = lax.axis_index("cell")
    slots = members * GROUP
    used = channels // CH
    rows = range(cells // GROUP)

    by_row = [[m * cells + y * GROUP + x for m in range(members) for x in range(GROUP)] for y in rows]

    def among_rows(move):
        return [(y * GROUP + x, move(y) * GROUP + x) for y in rows if move(y) in rows for x in range(GROUP)]

    def among_four(move):
        return [(y * GROUP + x, y * GROUP + move(x)) for y in rows for x in range(GROUP)]

    def exchange(to_left, to_right):
        return (
            lax.ppermute(to_right, "cell", among_rows(lambda y: y + 1)),
            lax.ppermute(to_left, "cell", among_rows(lambda y: y - 1)),
        )

    place = jnp.stack([cell // GROUP, cell % GROUP]).astype(jnp.int32)
    (send,) = call(pack_body, "pack", [shape(slots * CH * PER, LANE)])(preds)
    send, target, neighbours, area = lax.optimization_barrier((send, target, neighbours, area))
    recv = lax.all_to_all(
        send.reshape(slots, CH * PER, LANE), ("member", "cell"), 0, 0, axis_index_groups=by_row, tiled=True
    )

    by_slot = jnp.pad(target.astype(F32).reshape(CH, used, BLOCK), ((0, 0), (0, slots - used), (0, 0)))
    some = lax.dynamic_slice_in_dim(by_slot, member * GROUP, GROUP, 1)
    some = jnp.moveaxis(some, 1, 0).reshape(GROUP, CH * PER, LANE)
    common = jnp.concatenate([neighbours.astype(F32).reshape(NEIGH * PER, LANE), area.reshape(PER, LANE)])
    side = []
    for shift in range(GROUP):
        to = (cell + shift) % GROUP
        piece = jnp.concatenate([lax.dynamic_index_in_dim(some, to, 0, keepdims=False), common])
        if shift:
            piece = lax.ppermute(piece, "cell", among_four(lambda x: (x + shift) % GROUP))
        side.append(piece)
    side = jnp.stack(side)
    before, after = exchange(side, side)
    aux = jnp.concatenate([before, side, after])

    slot = member * GROUP + cell % GROUP
    weights = jnp.pad(channel_weight.reshape(CH, used), ((0, 0), (0, slots - used)))
    weights = lax.dynamic_index_in_dim(weights, slot, 1, keepdims=False)

    own, to_left, to_right = call(
        unpack_body,
        "unpack",
        [shape(CHUNKS, RF, LANE), shape(WIRE, LANE), shape(WIRE, LANE)],
        [pltpu.VMEM((CHUNKS * RF, LANE), F32), pltpu.VMEM((CHUNKS * RT + 16, LANE), F32)],
        scalars=1,
        vectors=2,
    )(place, recv, side)
    left, right = exchange(to_left, to_right)

    center, out_left, out_right, sums = call(
        functools.partial(main_body, cells * BLOCK),
        "smooth_score_back",
        [shape(CHUNKS, RB, LANE), shape(EDGE, RB, LANE), shape(EDGE, RB, LANE), shape(len(rows), PER, LANE)],
        [
            pltpu.VMEM((BLOCKS, BAND, TILE), BF16),
            pltpu.VMEM((2, 2 * RF, EXT), BF16),
            pltpu.VMEM((4 * 2 * BLOCKS * RF, LANE), F32),
            pltpu.VMEM((4 * CHUNKS * RB, LANE), F32),
            pltpu.VMEM((RB, EXT), F32),
            pltpu.VMEM((4 * PER, LANE), F32),
            pltpu.VMEM((2, BAND, TILE), BF16),
            pltpu.VMEM((2, BAND, TILE), BF16),
        ],
        scalars=2,
        vectors=4,
        limit=58,
    )(place, weights, own, left, right, aux)

    arrived = exchange(out_left, out_right)
    by_column = [[y * GROUP + x for y in rows] for x in range(GROUP)]
    sums = lax.all_to_all(sums, "cell", 0, 0, axis_index_groups=by_column, tiled=True)

    (packed,) = call(
        final_body,
        "gather_grad",
        [shape(slots * NOTE, LANE)],
        [pltpu.VMEM((CHUNKS * RB, LANE), F32)],
        vectors=4,
    )(center, *arrived, sums)
    back = lax.all_to_all(
        packed.reshape(slots, 1, NOTE * LANE), ("member", "cell"), 0, 0, axis_index_groups=by_row, tiled=True
    )
    losses, grad = call(spread_body, "spread", [shape(PER, LANE), shape(1, channels, BLOCK)], vectors=2)(
        back.reshape(slots * NOTE, LANE), jnp.pad(channel_weight, (0, LANE - channels)).reshape(1, LANE)
    )
    return losses[0, :4], grad


def solution(mesh):
    in_specs = (P("member", None, "cell"), P(None, "cell"), P("cell"), P(), P(None, "cell"))
    out_specs = (P(), P("member", None, "cell"))
    return jax.shard_map(local, mesh=mesh, in_specs=in_specs, out_specs=out_specs, check_vma=False)
```

time: 818 us -> 185 us (0.23)
  other arithmetic: 317 us -> 0.13 us
  local copies, waits for them, and re-layouts: 197 us -> 8.24 us
  blocking collectives: 108 us -> 15.3 us
  Pallas kernels: 0 us -> 77.6 us
  waiting for transfers between devices: 91.1 us -> 30.6 us
  starting transfers between devices: 92.9 us -> 51.5 us
    gather x4 -> x0, local copies, waits for them, and re-layouts: 118 us -> none  [smooth(): picked = jnp.take(extended, flat_index, axis=2)]
    scatter-add x12 -> x0, other arithmetic: 110 us -> none  [the longest x4 106 us: smooth_back(): extended = extended.at[:, :, flat_index].add(tiled)]
    psum x1 -> x0, blocking collectives: 108 us -> none  [local(): lax.psum((jnp.stack(numerators), jnp.sum(area_part)), ('member', 'cell'))]
    pallas_call x0 -> x5, Pallas kernels: none -> 77.6 us  [the longest x1 74.4 us: local(): call(functools.partial(main_body, cells * BLOCK), 'smooth_score_back', [s...]
    reduce_sum x27 -> x0, other arithmetic: 71.4 us -> none  [the longest x16 43.8 us: pair_group(): slope = jnp.sum(diff / root, axis=1)]
    select_n x5 -> x0, other arithmetic: 68 us -> none  [the longest x4 68 us: smooth(): picked = jnp.take(extended, flat_index, axis=2)]
    ppermute x16 -> x9, waiting for transfers between devices: 59.8 us -> 12.8 us  [the longest x3 5.11 us: exchange(): lax.ppermute(to_right, 'cell', among_rows(lambda y: y + 1))]
    concatenate x5 -> x0, other arithmetic: 45.9 us -> none  [the longest x4 43.3 us: padded(): block = jnp.concatenate([low, block, high], axis=dim)]
  transfers between devices with their start and end apart: 24 -> 11, of which waited for: 16 -> 4; matrix products, arithmetic and copies ran while one was open for 38% -> 1% of each run, Pallas kernels for 0% -> 0%
where the time goes in v1:
time: 185 us; the launch traced here: 184 us
  Pallas kernels  77.6 us (42%)
  starting transfers between devices  51.5 us (28%)
  waiting for transfers between devices  30.6 us (17%)
  blocking collectives  15.3 us (8%)
  local copies, waits for them, and re-layouts  8.24 us (4%)
    pallas_call x1, Pallas kernels, local(): call(functools.partial(main_body, cells * BLOCK), 'smooth_score_back', [s...  74.4 us
    all_to_all x1, waiting for transfers between devices, local(): lax.all_to_all(packed.reshape(slots, 1, NOTE * LANE), ('member', 'cell'),...  17.9 us
    all_to_all x1, blocking collectives, local(): lax.all_to_all(sums, 'cell', 0, 0, axis_index_groups=by_column, tiled=True)  15.3 us
    all_to_all x1, starting transfers between devices, local(): lax.all_to_all(send.reshape(slots, CH * PER, LANE), ('member', 'cell'), 0...  15 us
    all_to_all x1, starting transfers between devices, local(): lax.all_to_all(packed.reshape(slots, 1, NOTE * LANE), ('member', 'cell'),...  12 us
    ppermute x3, starting transfers between devices, exchange(): lax.ppermute(to_right, 'cell', among_rows(lambda y: y + 1))  10.6 us
    ppermute x3, starting transfers between devices, local(): lax.ppermute(piece, 'cell', among_four(lambda x: (x + shift) % GROUP))  10.1 us
    unnamed x27, local copies, waits for them, and re-layouts  6.79 us
  transfers between devices with their start and end apart: 11, of which 4 were waited for; matrix products, arithmetic and copies ran while one was open for 1% of the time, Pallas kernels for 0%

profile of v1, /device:TPU:1, one launch (start us, length us, event | category | flops | bytes accessed | tf_op | source)
XLA Modules:
  0.0 184.4 jit_solution(8419196024027935258)
XLA Ops:
  0.6 0.9 copy-done.2
  1.6 1.0 pack.1
  2.6 15.0 %all-to-all-start = ((f32[64,16,128]{2,1,0:T(8,128)}), f32[64,16,128]{2,1,0:T(8,128)S(1)}, u32[]{:S(2)}, u32[]{:S(2)}) async-start(f32[64,16,128]{2,1,0:T(8,128)} %bitcast.2), calls=%async_computation | async-start | bytes 1048576 | tf_op jit(solution)/shard_map/all_to_all | solution.py:415
  19.2 4.8 %collective-permute-start.1 = (f32[56,128]{1,0:T(8,128)S(1)}, f32[56,128]{1,0:T(8,128)S(1)}, u32[]{:S(2)}, u32[]{:S(2)}) collective-permute-start(f32[56,128]{1,0:T(8,128)S(1)} %get-tuple-element.42), channel_id=1, source_target_pairs={{0,2},{1,3},{2,0},{3,1},{4,6},{5,7},{6,4},{7,5},{8,10},{9,11},{10,... | collective-permute-start | bytes 86024 | tf_op jit(solution)/shard_map/ppermute | solution.py:428
  24.0 2.8 %collective-permute-start.2 = (f32[56,128]{1,0:T(8,128)S(1)}, f32[56,128]{1,0:T(8,128)S(1)}, u32[]{:S(2)}, u32[]{:S(2)}) collective-permute-start(f32[56,128]{1,0:T(8,128)S(1)} %get-tuple-element.43), channel_id=1, source_target_pairs={{0,3},{1,0},{2,1},{3,2},{4,7},{5,4},{6,5},{7,6},{8,11},{9,8},{10,9... | collective-permute-start | bytes 86024 | tf_op jit(solution)/shard_map/ppermute | solution.py:428
  26.8 2.5 %collective-permute-start = (f32[56,128]{1,0:T(8,128)S(1)}, f32[56,128]{1,0:T(8,128)S(1)}, u32[]{:S(2)}, u32[]{:S(2)}) collective-permute-start(f32[56,128]{1,0:T(8,128)S(1)} %get-tuple-element.41), channel_id=1, source_target_pairs={{0,1},{1,2},{2,3},{3,0},{4,5},{5,6},{6,7},{7,4},{8,9},{9,10},{10,1... | collective-permute-start | bytes 86024 | tf_op jit(solution)/shard_map/ppermute | solution.py:428
  29.3 3.8 %collective-permute-done = f32[56,128]{1,0:T(8,128)S(1)} collective-permute-done((f32[56,128]{1,0:T(8,128)S(1)}, f32[56,128]{1,0:T(8,128)S(1)}, u32[]{:S(2)}, u32[]{:S(2)}) %collective-permute-start) | collective-permute-done | bytes 28704 | tf_op jit(solution)/shard_map/ppermute | solution.py:428
  33.1 3.2 %collective-permute-start.5 = (f32[4,56,128]{2,1,0:T(8,128)S(1)}, f32[4,56,128]{2,1,0:T(8,128)S(1)}, u32[]{:S(2)}, u32[]{:S(2)}) collective-permute-start(f32[4,56,128]{2,1,0:T(8,128)S(1)} %pad_maximum_fusion.side_ref), channel_id=1, source_target_pairs={{0,4},{1,5},{2,6},{3,7},{4,8},{5,9},{6,10},{7,11},{8,12},{9,13},{1... | collective-permute-start | bytes 344072 | tf_op jit(solution)/shard_map/ppermute | solution.py:408
  37.9 1.3 collective-permute-start.6
  39.2 0.8 unpack.1
  40.1 0.8 copy-done
  40.9 4.0 %collective-permute-start.3 = (f32[792,128]{1,0:T(8,128)S(1)}, f32[792,128]{1,0:T(8,128)S(1)}, u32[]{:S(2)}, u32[]{:S(2)}) collective-permute-start(f32[792,128]{1,0:T(8,128)S(1)} %get-tuple-element.20), channel_id=1, source_target_pairs={{0,4},{1,5},{2,6},{3,7},{4,8},{5,9},{6,10},{7,11},{8,12},{9,13},{1... | collective-permute-start | bytes 1216520 | tf_op jit(solution)/shard_map/ppermute | solution.py:408
  44.9 1.3 collective-permute-start.4
  46.3 5.1 %collective-permute-done.3.left_ref = f32[792,128]{1,0:T(8,128)S(1)} collective-permute-done((f32[792,128]{1,0:T(8,128)S(1)}, f32[792,128]{1,0:T(8,128)S(1)}, u32[]{:S(2)}, u32[]{:S(2)}) %collective-permute-start.3) | collective-permute-done | bytes 405536 | tf_op jit(solution)/shard_map/ppermute | solution.py:408
  51.4 3.9 %collective-permute-done.4.right_ref = f32[792,128]{1,0:T(8,128)S(1)} collective-permute-done((f32[792,128]{1,0:T(8,128)S(1)}, f32[792,128]{1,0:T(8,128)S(1)}, u32[]{:S(2)}, u32[]{:S(2)}) %collective-permute-start.4) | collective-permute-done | bytes 405536 | tf_op jit(solution)/shard_map/ppermute | solution.py:409
  56.0 74.4 %smooth_score_back.1 = (f32[32,32,128]{2,1,0:T(8,128)}, f32[23,32,128]{2,1,0:T(8,128)}, f32[23,32,128]{2,1,0:T(8,128)}, f32[8,8,128]{2,1,0:T(8,128)}) custom-call(s32[2]{0:T(128)} %copy-done.3, f32[2]{0:T(128)} %fusion.1.weight_ref, f32[32,40,128]{2,1,0:T(8,128)} %copy-done, f32[792,128]{1,0:T(8,128)} %copy-done.5, f32[792,128]{1,0:T(8,128)} %copy-done.6, ...), custom_call_target="tpu_custom_call" | custom-call | tf_op jit(solution)/shard_map/smooth_score_back/pallas_call | solution.py:448
  130.4 3.4 %collective-permute-start.7 = (f32[23,32,128]{2,1,0:T(8,128)}, f32[23,32,128]{2,1,0:T(8,128)S(1)}, u32[]{:S(2)}, u32[]{:S(2)}) collective-permute-start(f32[23,32,128]{2,1,0:T(8,128)} %get-tuple-element.23), channel_id=1, source_target_pairs={{0,4},{1,5},{2,6},{3,7},{4,8},{5,9},{6,10},{7,11},{8,12},{9,13},{1... | collective-permute-start | bytes 1130504 | tf_op jit(solution)/shard_map/ppermute | solution.py:408
  133.8 1.3 collective-permute-start.8
  135.1 15.3 %all_to_all.15.sums_ref = f32[8,8,128]{2,1,0:T(8,128)S(1)} all-to-all(f32[8,8,128]{2,1,0:T(8,128)} %get-tuple-element.25), channel_id=1, replica_groups={{0,4,8,12,16,20,24,28},{1,5,9,13,17,21,25,29},{2,6,10,14,18,22,26,30},{..., dimensions={0} | all-to-all | bytes 65536 | tf_op jit(solution)/shard_map/all_to_all | solution.py:469
  150.5 1.0 copy-done.1
  151.5 1.3 gather_grad.1
  152.8 12.0 %all-to-all-start.2 = ((f32[64,1,2176]{2,1,0:T(1,128)}), f32[64,1,2176]{2,1,0:T(1,128)S(1)}, u32[]{:S(2)}, u32[]{:S(2)}) async-start(f32[64,1,2176]{2,1,0:T(1,128)} %bitcast.13), calls=%async_computation.2 | async-start | bytes 1114112 | tf_op jit(solution)/shard_map/all_to_all | solution.py:478
  164.8 17.9 %all-to-all-done.2 = f32[64,1,2176]{2,1,0:T(1,128)S(1)} async-done(((f32[64,1,2176]{2,1,0:T(1,128)}), f32[64,1,2176]{2,1,0:T(1,128)S(1)}, u32[]{:S(2)}, u32[]{:S(2)}) %all-to-all-start.2) | async-done | bytes 557088 | tf_op jit(solution)/shard_map/all_to_all | solution.py:478
  182.7 1.2 copy.14
  (47 shorter events, 4.5 us)
Async XLA Ops:
  0.6 0.9 copy-start.2
  2.6 15.0 %copy-start.7 = (bf16[100,1024]{1,0:T(8,128)(2,1)S(1)}, bf16[100,1024]{1,0:T(8,128)(2,1)}, u32[]{:S(2)}) copy-start(bf16[100,1024]{1,0:T(8,128)(2,1)} %param.6) | copy-start | bytes 614404
  2.6 36.7 %all-to-all-start = ((f32[64,16,128]{2,1,0:T(8,128)}), f32[64,16,128]{2,1,0:T(8,128)S(1)}, u32[]{:S(2)}, u32[]{:S(2)}) async-start(f32[64,16,128]{2,1,0:T(8,128)} %bitcast.2), calls=%async_computation | async-start | bytes 1048576 | tf_op jit(solution)/shard_map/all_to_all | solution.py:415
  17.7 0.7 copy-start.8
  18.5 0.7 copy-start.9
  19.2 10.1 %collective-permute-start.1 = (f32[56,128]{1,0:T(8,128)S(1)}, f32[56,128]{1,0:T(8,128)S(1)}, u32[]{:S(2)}, u32[]{:S(2)}) collective-permute-start(f32[56,128]{1,0:T(8,128)S(1)} %get-tuple-element.42), channel_id=1, source_target_pairs={{0,2},{1,3},{2,0},{3,1},{4,6},{5,7},{6,4},{7,5},{8,10},{9,11},{10,... | collective-permute-start | bytes 86024 | tf_op jit(solution)/shard_map/ppermute | solution.py:428
  24.0 5.3 %collective-permute-start.2 = (f32[56,128]{1,0:T(8,128)S(1)}, f32[56,128]{1,0:T(8,128)S(1)}, u32[]{:S(2)}, u32[]{:S(2)}) collective-permute-start(f32[56,128]{1,0:T(8,128)S(1)} %get-tuple-element.43), channel_id=1, source_target_pairs={{0,3},{1,0},{2,1},{3,2},{4,7},{5,4},{6,5},{7,6},{8,11},{9,8},{10,9... | collective-permute-start | bytes 86024 | tf_op jit(solution)/shard_map/ppermute | solution.py:428
  26.8 6.3 %collective-permute-start = (f32[56,128]{1,0:T(8,128)S(1)}, f32[56,128]{1,0:T(8,128)S(1)}, u32[]{:S(2)}, u32[]{:S(2)}) collective-permute-start(f32[56,128]{1,0:T(8,128)S(1)} %get-tuple-element.41), channel_id=1, source_target_pairs={{0,1},{1,2},{2,3},{3,0},{4,5},{5,6},{6,7},{7,4},{8,9},{9,10},{10,1... | collective-permute-start | bytes 86024 | tf_op jit(solution)/shard_map/ppermute | solution.py:428
  33.1 6.1 %collective-permute-start.5 = (f32[4,56,128]{2,1,0:T(8,128)S(1)}, f32[4,56,128]{2,1,0:T(8,128)S(1)}, u32[]{:S(2)}, u32[]{:S(2)}) collective-permute-start(f32[4,56,128]{2,1,0:T(8,128)S(1)} %pad_maximum_fusion.side_ref), channel_id=1, source_target_pairs={{0,4},{1,5},{2,6},{3,7},{4,8},{5,9},{6,10},{7,11},{8,12},{9,13},{1... | collective-permute-start | bytes 344072 | tf_op jit(solution)/shard_map/ppermute | solution.py:408
  36.4 0.7 copy-start.10
  37.9 1.4 copy-start.3
  37.9 8.4 %collective-permute-start.6 = (f32[4,56,128]{2,1,0:T(8,128)S(1)}, f32[4,56,128]{2,1,0:T(8,128)S(1)}, u32[]{:S(2)}, u32[]{:S(2)}) collective-permute-start(f32[4,56,128]{2,1,0:T(8,128)S(1)} %pad_maximum_fusion.side_ref), channel_id=1, source_target_pairs={{4,0},{5,1},{6,2},{7,3},{8,4},{9,5},{10,6},{11,7},{12,8},{13,9},{1... | collective-permute-start | bytes 344072 | tf_op jit(solution)/shard_map/ppermute | solution.py:409
  40.1 0.9 copy-start
  40.9 10.5 %collective-permute-start.3 = (f32[792,128]{1,0:T(8,128)S(1)}, f32[792,128]{1,0:T(8,128)S(1)}, u32[]{:S(2)}, u32[]{:S(2)}) collective-permute-start(f32[792,128]{1,0:T(8,128)S(1)} %get-tuple-element.20), channel_id=1, source_target_pairs={{0,4},{1,5},{2,6},{3,7},{4,8},{5,9},{6,10},{7,11},{8,12},{9,13},{1... | collective-permute-start | bytes 1216520 | tf_op jit(solution)/shard_map/ppermute | solution.py:408
  44.9 10.3 %collective-permute-start.4 = (f32[792,128]{1,0:T(8,128)S(1)}, f32[792,128]{1,0:T(8,128)S(1)}, u32[]{:S(2)}, u32[]{:S(2)}) collective-permute-start(f32[792,128]{1,0:T(8,128)S(1)} %get-tuple-element.21), channel_id=1, source_target_pairs={{4,0},{5,1},{6,2},{7,3},{8,4},{9,5},{10,6},{11,7},{12,8},{13,9},{1... | collective-permute-start | bytes 1216520 | tf_op jit(solution)/shard_map/ppermute | solution.py:409
  46.3 9.0 %copy-start.4 = (f32[12,56,128]{2,1,0:T(8,128)}, f32[12,56,128]{2,1,0:T(8,128)S(1)}, u32[]{:S(2)}) copy-start(f32[12,56,128]{2,1,0:T(8,128)S(1)} %constant_dynamic-update-slice_fusion.aux_ref) | copy-start | bytes 1032196
  51.4 3.9 %copy-start.5 = (f32[792,128]{1,0:T(8,128)}, f32[792,128]{1,0:T(8,128)S(1)}, u32[]{:S(2)}) copy-start(f32[792,128]{1,0:T(8,128)S(1)} %collective-permute-done.3.left_ref) | copy-start | bytes 1216516
  55.3 0.8 copy-start.6
  130.4 20.1 %collective-permute-start.7 = (f32[23,32,128]{2,1,0:T(8,128)}, f32[23,32,128]{2,1,0:T(8,128)S(1)}, u32[]{:S(2)}, u32[]{:S(2)}) collective-permute-start(f32[23,32,128]{2,1,0:T(8,128)} %get-tuple-element.23), channel_id=1, source_target_pairs={{0,4},{1,5},{2,6},{3,7},{4,8},{5,9},{6,10},{7,11},{8,12},{9,13},{1... | collective-permute-start | bytes 1130504 | tf_op jit(solution)/shard_map/ppermute | solution.py:408
  133.8 16.6 %collective-permute-start.8 = (f32[23,32,128]{2,1,0:T(8,128)}, f32[23,32,128]{2,1,0:T(8,128)S(1)}, u32[]{:S(2)}, u32[]{:S(2)}) collective-permute-start(f32[23,32,128]{2,1,0:T(8,128)} %get-tuple-element.24), channel_id=1, source_target_pairs={{4,0},{5,1},{6,2},{7,3},{8,4},{9,5},{10,6},{11,7},{12,8},{13,9},{1... | collective-permute-start | bytes 1130504 | tf_op jit(solution)/shard_map/ppermute | solution.py:409
  150.5 1.0 copy-start.1
  152.8 29.8 %all-to-all-start.2 = ((f32[64,1,2176]{2,1,0:T(1,128)}), f32[64,1,2176]{2,1,0:T(1,128)S(1)}, u32[]{:S(2)}, u32[]{:S(2)}) async-start(f32[64,1,2176]{2,1,0:T(1,128)} %bitcast.13), calls=%async_computation.2 | async-start | bytes 1114112 | tf_op jit(solution)/shard_map/all_to_all | solution.py:478

commit v2 on v1

--- a/solution.py
+++ b/solution.py
@@ -99,19 +99,22 @@
     return pl.ds(pl.multiple_of(index * TILE, TILE), count * TILE)
 
 
-def builder(row_group, mine, aux_ref, band, cells):
-    down = lax.broadcasted_iota(jnp.int32, (TILE, TILE), 0)
-    across = lax.broadcasted_iota(jnp.int32, (TILE, TILE), 1)
-    unit = jnp.where(down == across, 0.5, 0.0).astype(BF16)
-    count = down.astype(F32).astype(BF16)
-    weight = jnp.full((TILE, TILE), 0.5 / NEIGH, BF16)
-    none = jnp.zeros((TILE, TILE), BF16)
+def builder(row_group, mine, aux_ref, band, pattern, cells):
+    down = lax.broadcasted_iota(jnp.int32, (TILE, TILE), 0).astype(F32)
+    across = lax.broadcasted_iota(jnp.int32, (1, TILE), 1).astype(F32)
+    share = 0.5 / NEIGH
     first_cell = row_group * WIDTH - SIDE * TILE
-
-    def hits(relative, t):
-        at = relative - float(t * TILE)
-        at = jnp.where((at < 0.0) | (at > TILE - 1.0), -1.0, at).astype(BF16)
-        return jnp.where(count == at, weight, none)
+    own = REACH * TILE
+    fixed = (own - ROW, own + ROW)
+
+    def hits(place, t):
+        return jnp.where(down == place - float(t * TILE), share, 0.0)
+
+    for t in range(2 * REACH + 1):
+        total = hits(across + float(fixed[0]), t) + hits(across + float(fixed[1]), t)
+        if t == REACH:
+            total = total + NEIGH * hits(across + float(own), t)
+        pattern[t * TILE : (t + 1) * TILE, :] = total.astype(BF16)
 
     def places(b, k):
         halves = []
@@ -123,37 +126,39 @@
         return jnp.concatenate(halves, axis=1) - (first_cell + b * TILE).astype(F32)
 
     def plain(b, h, stage):
-        relative = [places(b, k) for k in range(NEIGH)]
-        for t in range(2 * REACH + 1):
-            total = hits(relative[2], t) + hits(relative[3], t)
-            if t < 2:
-                total = total + hits(relative[0], t)
-            if t > 2 * REACH - 2:
-                total = total + hits(relative[1], t)
-            if t == REACH:
-                total = total + unit
-            span = slice(t * TILE, (t + 1) * TILE)
+        near, far = [], []
+        for k in (2, 3):
+            place = places(b, k)
+            high = jnp.floor(place * (1.0 / LANE))
+            near.append(jnp.where(down[:LANE] == place - high * LANE, share, 0.0).astype(BF16))
+            far.append(high)
+        for t in range(BAND // LANE):
+            span = slice(t * LANE, (t + 1) * LANE)
+            total = pattern[span, :]
+            for k in range(2):
+                total = total + near[k] * jnp.where(far[k] == float(t), 1.0, 0.0).astype(BF16)
             stage[h, span, :] = total
             band[b, span, :] = total
 
     def clipped(b, h, stage):
         cell = first_cell + (b + REACH) * TILE
 
-        def more(k, tiles):
-            relative = places(b, k)
-            for t in tiles:
+        def correct(k):
+            place = places(b, k)
+            for t in range(2 * REACH + 1):
                 span = slice(t * TILE, (t + 1) * TILE)
-                total = band[b, span, :] + hits(relative, t)
+                change = hits(place, t) - hits(across + float(fixed[k]), t)
+                total = band[b, span, :] + change.astype(BF16)
                 stage[h, span, :] = total
                 band[b, span, :] = total
 
-        @pl.when(cell < ROW)
+        @pl.when((cell >= 0) & (cell < ROW))
         def _():
-            more(0, range(2, 2 * REACH + 1))
-
-        @pl.when(cell + TILE > cells - ROW)
+            correct(0)
+
+        @pl.when((cell < cells) & (cell + TILE > cells - ROW))
         def _():
-            more(1, range(2 * REACH - 1))
+            correct(1)
 
     return plain, clipped
 
@@ -200,11 +205,11 @@
 
 def main_body(
     cells, place_ref, weight_ref, own_ref, left_ref, right_ref, aux_ref,
-    center_ref, outl_ref, outr_ref, loss_ref, band, xs, rows, slopes, total, sums, stage_a, stage_b,
+    center_ref, outl_ref, outr_ref, loss_ref, band, xs, rows, slopes, total, sums, stage_a, stage_b, pattern,
 ):
     row_group = place_ref[0]
     mine = place_ref[1]
-    plain, clipped = builder(row_group, mine, aux_ref, band, cells)
+    plain, clipped = builder(row_group, mine, aux_ref, band, pattern, cells)
     score = scorer(weight_ref, mine, aux_ref, rows, slopes, sums)
 
     xs[0, :, :LANE] = jnp.zeros((2 * RF, LANE), BF16)
@@ -331,9 +336,13 @@
                         preferred_element_type=F32,
                     )
                 )
-            for h in range(2):
-                at = tile_at(2 * p + h + first, 2 * REACH + 1)
-                total[:, at] = total[:, at] + (got[h][:RB] + got[h][RB:])
+            one, two = (value[:RB] + value[RB:] for value in got)
+            at = tile_at(2 * p + first)
+            total[:, at] = total[:, at] + one[:, :TILE]
+            at = tile_at(2 * p + first + 1, 2 * REACH)
+            total[:, at] = total[:, at] + (one[:, TILE:] + two[:, :-TILE])
+            at = tile_at(2 * p + first + 2 * REACH + 1)
+            total[:, at] = total[:, at] + two[:, -TILE:]
             return carry
 
         lax.fori_loop(0, (BLOCKS - 2 * first) // 2, backward, 0)
@@ -377,12 +386,14 @@
     lane = lax.broadcasted_iota(jnp.int32, (1, LANE), 1)
     area = jnp.sum(jnp.where(lane == 4, sums, 0.0), axis=1, keepdims=True)
     scale = 1.0 / (jnp.sum(weight_ref[...], axis=1, keepdims=True) * area)
-    losses_ref[...] = jnp.broadcast_to(sums * scale, losses_ref.shape)
-    used = out_ref.shape[1] // CH
+    losses = sums * scale
+    for level in range(losses_ref.shape[0]):
+        losses_ref[level] = losses[0, level]
+    used = out_ref.shape[0] // (CH * PER)
     for c in range(CH):
-        for l in range(PER):
-            part = recv_ref[pl.ds(c * PER + l, used, stride=NOTE), :]
-            out_ref[0, c * used : (c + 1) * used, l * LANE : (l + 1) * LANE] = part * scale
+        for q in range(used):
+            part = recv_ref[q * NOTE + c * PER : q * NOTE + (c + 1) * PER, :]
+            out_ref[(c * used + q) * PER : (c * used + q + 1) * PER, :] = part * scale
 
 
 def local(preds, target, area, channel_weight, neighbours):
@@ -428,9 +439,6 @@
             piece = lax.ppermute(piece, "cell", among_four(lambda x: (x + shift) % GROUP))
         side.append(piece)
     side = jnp.stack(side)
-    before, after = exchange(side, side)
-    aux = jnp.concatenate([before, side, after])
-
     slot = member * GROUP + cell % GROUP
     weights = jnp.pad(channel_weight.reshape(CH, used), ((0, 0), (0, slots - used)))
     weights = lax.dynamic_index_in_dim(weights, slot, 1, keepdims=False)
@@ -443,7 +451,10 @@
         scalars=1,
         vectors=2,
     )(place, recv, side)
+    own, side, to_left, to_right = lax.optimization_barrier((own, side, to_left, to_right))
     left, right = exchange(to_left, to_right)
+    before, after = exchange(side, side)
+    aux = jnp.concatenate([before, side, after])
 
     center, out_left, out_right, sums = call(
         functools.partial(main_body, cells * BLOCK),
@@ -458,6 +469,7 @@
             pltpu.VMEM((4 * PER, LANE), F32),
             pltpu.VMEM((2, BAND, TILE), BF16),
             pltpu.VMEM((2, BAND, TILE), BF16),
+            pltpu.VMEM((BAND, TILE), BF16),
         ],
         scalars=2,
         vectors=4,
@@ -478,10 +490,15 @@
     back = lax.all_to_all(
         packed.reshape(slots, 1, NOTE * LANE), ("member", "cell"), 0, 0, axis_index_groups=by_row, tiled=True
     )
-    losses, grad = call(spread_body, "spread", [shape(PER, LANE), shape(1, channels, BLOCK)], vectors=2)(
-        back.reshape(slots * NOTE, LANE), jnp.pad(channel_weight, (0, LANE - channels)).reshape(1, LANE)
-    )
-    return losses[0, :4], grad
+    losses, grad = pl.pallas_call(
+        spread_body,
+        in_specs=[VMEM_SPEC] * 2,
+        out_specs=[SMEM_SPEC, VMEM_SPEC],
+        out_shape=[shape(4), shape(channels * PER, LANE)],
+        compiler_params=pltpu.CompilerParams(vmem_limit_bytes=24 * 1024 * 1024),
+        name="spread",
+    )(back.reshape(slots * NOTE, LANE), jnp.pad(channel_weight, (0, LANE - channels)).reshape(1, LANE))
+    return losses, grad.reshape(1, channels, BLOCK)
 
 
 def solution(mesh):

time: 185 us -> 181 us (0.978)
  starting transfers between devices: 51.5 us -> 48.6 us
  waiting for transfers between devices: 30.6 us -> 28.3 us
    ppermute x3, waiting for transfers between devices: 5.11 us -> 1.24 us  [exchange(): lax.ppermute(to_right, 'cell', among_rows(lambda y: y + 1))]
    all_to_all x1, starting transfers between devices: 12 us -> 9.81 us  [local(): lax.all_to_all(packed.reshape(slots, 1, NOTE * LANE), ('member', 'cell'),...]
    unnamed x27 -> x20, local copies, waits for them, and re-layouts: 6.79 us -> 6.34 us
  transfers between devices with their start and end apart: 11 -> 11, of which waited for: 4 -> 5; matrix products, arithmetic and copies ran while one was open for 1% -> 1% of each run, Pallas kernels for 0% -> 0%
where the time goes in v2:
time: 181 us; the launch traced here: 180 us
  Pallas kernels  78.2 us (43%)
  starting transfers between devices  48.6 us (27%)
  waiting for transfers between devices  28.3 us (16%)
  blocking collectives  15.9 us (9%)
  local copies, waits for them, and re-layouts  7.25 us (4%)
    pallas_call x1, Pallas kernels, local(): call(functools.partial(main_body, cells * BLOCK), 'smooth_score_back', [s...  74.2 us
    all_to_all x1, waiting for transfers between devices, local(): lax.all_to_all(packed.reshape(slots, 1, NOTE * LANE), ('member', 'cell'),...  17.9 us
    all_to_all x1, blocking collectives, local(): lax.all_to_all(sums, 'cell', 0, 0, axis_index_groups=by_column, tiled=True)  15.9 us
    all_to_all x1, starting transfers between devices, local(): lax.all_to_all(send.reshape(slots, CH * PER, LANE), ('member', 'cell'), 0...  15 us
    ppermute x3, starting transfers between devices, local(): lax.ppermute(piece, 'cell', among_four(lambda x: (x + shift) % GROUP))  10.1 us
    ppermute x3, starting transfers between devices, exchange(): lax.ppermute(to_right, 'cell', among_rows(lambda y: y + 1))  9.86 us
    all_to_all x1, starting transfers between devices, local(): lax.all_to_all(packed.reshape(slots, 1, NOTE * LANE), ('member', 'cell'),...  9.81 us
    unnamed x20, local copies, waits for them, and re-layouts  6.34 us
  transfers between devices with their start and end apart: 11, of which 5 were waited for; matrix products, arithmetic and copies ran while one was open for 1% of the time, Pallas kernels for 0%

profile of v2, /device:TPU:1, one launch (start us, length us, event | category | flops | bytes accessed | tf_op | source)
XLA Modules:
  0.0 180.3 jit_solution(2776593117645945924)
XLA Ops:
  0.6 0.9 copy-done.2
  1.6 1.0 pack.1
  2.6 15.0 %all-to-all-start = ((f32[64,16,128]{2,1,0:T(8,128)}), f32[64,16,128]{2,1,0:T(8,128)S(1)}, u32[]{:S(2)}, u32[]{:S(2)}) async-start(f32[64,16,128]{2,1,0:T(8,128)} %bitcast.2), calls=%async_computation | async-start | bytes 1048576 | tf_op jit(solution)/shard_map/all_to_all | solution.py:426
  19.2 4.8 %collective-permute-start.1 = (f32[56,128]{1,0:T(8,128)S(1)}, f32[56,128]{1,0:T(8,128)S(1)}, u32[]{:S(2)}, u32[]{:S(2)}) collective-permute-start(f32[56,128]{1,0:T(8,128)S(1)} %get-tuple-element.50), channel_id=1, source_target_pairs={{0,2},{1,3},{2,0},{3,1},{4,6},{5,7},{6,4},{7,5},{8,10},{9,11},{10,... | collective-permute-start | bytes 86024 | tf_op jit(solution)/shard_map/ppermute | solution.py:439
  24.0 2.8 %collective-permute-start.2 = (f32[56,128]{1,0:T(8,128)S(1)}, f32[56,128]{1,0:T(8,128)S(1)}, u32[]{:S(2)}, u32[]{:S(2)}) collective-permute-start(f32[56,128]{1,0:T(8,128)S(1)} %get-tuple-element.51), channel_id=1, source_target_pairs={{0,3},{1,0},{2,1},{3,2},{4,7},{5,4},{6,5},{7,6},{8,11},{9,8},{10,9... | collective-permute-start | bytes 86024 | tf_op jit(solution)/shard_map/ppermute | solution.py:439
  26.8 2.5 %collective-permute-start = (f32[56,128]{1,0:T(8,128)S(1)}, f32[56,128]{1,0:T(8,128)S(1)}, u32[]{:S(2)}, u32[]{:S(2)}) collective-permute-start(f32[56,128]{1,0:T(8,128)S(1)} %get-tuple-element.49), channel_id=1, source_target_pairs={{0,1},{1,2},{2,3},{3,0},{4,5},{5,6},{6,7},{7,4},{8,9},{9,10},{10,1... | collective-permute-start | bytes 86024 | tf_op jit(solution)/shard_map/ppermute | solution.py:439
  29.4 3.7 %collective-permute-done = f32[56,128]{1,0:T(8,128)S(1)} collective-permute-done((f32[56,128]{1,0:T(8,128)S(1)}, f32[56,128]{1,0:T(8,128)S(1)}, u32[]{:S(2)}, u32[]{:S(2)}) %collective-permute-start) | collective-permute-done | bytes 28704 | tf_op jit(solution)/shard_map/ppermute | solution.py:439
  33.1 1.7 all-to-all-done.recv_ref
  35.6 0.8 copy-done
  36.5 3.2 %collective-permute-start.3 = (f32[792,128]{1,0:T(8,128)S(1)}, f32[792,128]{1,0:T(8,128)S(1)}, u32[]{:S(2)}, u32[]{:S(2)}) collective-permute-start(f32[792,128]{1,0:T(8,128)S(1)} %get-tuple-element.27), channel_id=1, source_target_pairs={{0,4},{1,5},{2,6},{3,7},{4,8},{5,9},{6,10},{7,11},{8,12},{9,13},{1... | collective-permute-start | bytes 1216520 | tf_op jit(solution)/shard_map/ppermute | solution.py:419
  39.7 1.3 collective-permute-start.4
  41.0 4.0 %collective-permute-start.5 = (f32[4,56,128]{2,1,0:T(8,128)S(1)}, f32[4,56,128]{2,1,0:T(8,128)S(1)}, u32[]{:S(2)}, u32[]{:S(2)}) collective-permute-start(f32[4,56,128]{2,1,0:T(8,128)S(1)} %pad_maximum_fusion.1.side_ref), channel_id=1, source_target_pairs={{0,4},{1,5},{2,6},{3,7},{4,8},{5,9},{6,10},{7,11},{8,12},{9,13},{1... | collective-permute-start | bytes 344072 | tf_op jit(solution)/shard_map/ppermute | solution.py:419
  45.0 1.3 collective-permute-start.6
  47.8 1.2 collective-permute-done.5
  49.0 3.9 %collective-permute-done.6 = f32[4,56,128]{2,1,0:T(8,128)S(1)} collective-permute-done((f32[4,56,128]{2,1,0:T(8,128)S(1)}, f32[4,56,128]{2,1,0:T(8,128)S(1)}, u32[]{:S(2)}, u32[]{:S(2)}) %collective-permute-start.6) | collective-permute-done | bytes 114720 | tf_op jit(solution)/shard_map/ppermute | solution.py:420
  55.1 74.2 %smooth_score_back.1 = (f32[32,32,128]{2,1,0:T(8,128)}, f32[23,32,128]{2,1,0:T(8,128)}, f32[23,32,128]{2,1,0:T(8,128)}, f32[8,8,128]{2,1,0:T(8,128)}) custom-call(s32[2]{0:T(128)} %copy-done.3, f32[2]{0:T(128)} %fusion.1.weight_ref, f32[32,40,128]{2,1,0:T(8,128)} %copy-done, f32[792,128]{1,0:T(8,128)} %copy-done.4, f32[792,128]{1,0:T(8,128)} %copy-done.5, ...), custom_call_target="tpu_custom_call" | custom-call | tf_op jit(solution)/shard_map/smooth_score_back/pallas_call | solution.py:459
  129.4 2.7 %collective-permute-start.7 = (f32[23,32,128]{2,1,0:T(8,128)}, f32[23,32,128]{2,1,0:T(8,128)S(1)}, u32[]{:S(2)}, u32[]{:S(2)}) collective-permute-start(f32[23,32,128]{2,1,0:T(8,128)} %get-tuple-element.31), channel_id=1, source_target_pairs={{0,4},{1,5},{2,6},{3,7},{4,8},{5,9},{6,10},{7,11},{8,12},{9,13},{1... | collective-permute-start | bytes 1130504 | tf_op jit(solution)/shard_map/ppermute | solution.py:419
  132.0 1.3 collective-permute-start.8
  133.3 15.9 %all_to_all.15.sums_ref = f32[8,8,128]{2,1,0:T(8,128)S(1)} all-to-all(f32[8,8,128]{2,1,0:T(8,128)} %get-tuple-element.33), channel_id=1, replica_groups={{0,4,8,12,16,20,24,28},{1,5,9,13,17,21,25,29},{2,6,10,14,18,22,26,30},{..., dimensions={0} | all-to-all | bytes 65536 | tf_op jit(solution)/shard_map/all_to_all | solution.py:481
  149.2 1.0 copy-done.1
  150.3 1.3 gather_grad.1
  151.5 9.8 %all-to-all-start.2 = ((f32[64,1,2176]{2,1,0:T(1,128)}), f32[64,1,2176]{2,1,0:T(1,128)S(1)}, u32[]{:S(2)}, u32[]{:S(2)}) async-start(f32[64,1,2176]{2,1,0:T(1,128)} %bitcast.13), calls=%async_computation.2 | async-start | bytes 1114112 | tf_op jit(solution)/shard_map/all_to_all | solution.py:490
  161.4 17.9 %all-to-all-done.2 = f32[64,1,2176]{2,1,0:T(1,128)S(1)} async-done(((f32[64,1,2176]{2,1,0:T(1,128)}), f32[64,1,2176]{2,1,0:T(1,128)S(1)}, u32[]{:S(2)}, u32[]{:S(2)}) %all-to-all-start.2) | async-done | bytes 557088 | tf_op jit(solution)/shard_map/all_to_all | solution.py:490
  179.2 0.9 spread.1
  (38 shorter events, 6.2 us)
Async XLA Ops:
  0.6 0.9 copy-start.2
  2.6 15.0 %copy-start.6 = (bf16[100,1024]{1,0:T(8,128)(2,1)S(1)}, bf16[100,1024]{1,0:T(8,128)(2,1)}, u32[]{:S(2)}) copy-start(bf16[100,1024]{1,0:T(8,128)(2,1)} %param.6) | copy-start | bytes 614404
  2.6 32.2 %all-to-all-start = ((f32[64,16,128]{2,1,0:T(8,128)}), f32[64,16,128]{2,1,0:T(8,128)S(1)}, u32[]{:S(2)}, u32[]{:S(2)}) async-start(f32[64,16,128]{2,1,0:T(8,128)} %bitcast.2), calls=%async_computation | async-start | bytes 1048576 | tf_op jit(solution)/shard_map/all_to_all | solution.py:426
  17.7 0.7 copy-start.7
  18.5 0.7 copy-start.8
  19.2 10.2 %collective-permute-start.1 = (f32[56,128]{1,0:T(8,128)S(1)}, f32[56,128]{1,0:T(8,128)S(1)}, u32[]{:S(2)}, u32[]{:S(2)}) collective-permute-start(f32[56,128]{1,0:T(8,128)S(1)} %get-tuple-element.50), channel_id=1, source_target_pairs={{0,2},{1,3},{2,0},{3,1},{4,6},{5,7},{6,4},{7,5},{8,10},{9,11},{10,... | collective-permute-start | bytes 86024 | tf_op jit(solution)/shard_map/ppermute | solution.py:439
  24.0 5.4 %collective-permute-start.2 = (f32[56,128]{1,0:T(8,128)S(1)}, f32[56,128]{1,0:T(8,128)S(1)}, u32[]{:S(2)}, u32[]{:S(2)}) collective-permute-start(f32[56,128]{1,0:T(8,128)S(1)} %get-tuple-element.51), channel_id=1, source_target_pairs={{0,3},{1,0},{2,1},{3,2},{4,7},{5,4},{6,5},{7,6},{8,11},{9,8},{10,9... | collective-permute-start | bytes 86024 | tf_op jit(solution)/shard_map/ppermute | solution.py:439
  26.8 6.3 %collective-permute-start = (f32[56,128]{1,0:T(8,128)S(1)}, f32[56,128]{1,0:T(8,128)S(1)}, u32[]{:S(2)}, u32[]{:S(2)}) collective-permute-start(f32[56,128]{1,0:T(8,128)S(1)} %get-tuple-element.49), channel_id=1, source_target_pairs={{0,1},{1,2},{2,3},{3,0},{4,5},{5,6},{6,7},{7,4},{8,9},{9,10},{10,1... | collective-permute-start | bytes 86024 | tf_op jit(solution)/shard_map/ppermute | solution.py:439
  29.4 5.4 %copy-start.3 = (s32[2]{0:T(128)}, s32[2]{0:T(128)S(1)}, u32[]{:S(2)}) copy-start(s32[2]{0:T(128)S(1)} %pad_add_fusion.place_ref) | copy-start | bytes 28
  35.6 0.9 copy-start
  36.5 17.1 %collective-permute-start.3 = (f32[792,128]{1,0:T(8,128)S(1)}, f32[792,128]{1,0:T(8,128)S(1)}, u32[]{:S(2)}, u32[]{:S(2)}) collective-permute-start(f32[792,128]{1,0:T(8,128)S(1)} %get-tuple-element.27), channel_id=1, source_target_pairs={{0,4},{1,5},{2,6},{3,7},{4,8},{5,9},{6,10},{7,11},{8,12},{9,13},{1... | collective-permute-start | bytes 1216520 | tf_op jit(solution)/shard_map/ppermute | solution.py:419
  39.7 13.9 %collective-permute-start.4 = (f32[792,128]{1,0:T(8,128)S(1)}, f32[792,128]{1,0:T(8,128)S(1)}, u32[]{:S(2)}, u32[]{:S(2)}) collective-permute-start(f32[792,128]{1,0:T(8,128)S(1)} %get-tuple-element.28), channel_id=1, source_target_pairs={{4,0},{5,1},{6,2},{7,3},{8,4},{9,5},{10,6},{11,7},{12,8},{13,9},{1... | collective-permute-start | bytes 1216520 | tf_op jit(solution)/shard_map/ppermute | solution.py:420
  41.0 8.0 %collective-permute-start.5 = (f32[4,56,128]{2,1,0:T(8,128)S(1)}, f32[4,56,128]{2,1,0:T(8,128)S(1)}, u32[]{:S(2)}, u32[]{:S(2)}) collective-permute-start(f32[4,56,128]{2,1,0:T(8,128)S(1)} %pad_maximum_fusion.1.side_ref), channel_id=1, source_target_pairs={{0,4},{1,5},{2,6},{3,7},{4,8},{5,9},{6,10},{7,11},{8,12},{9,13},{1... | collective-permute-start | bytes 344072 | tf_op jit(solution)/shard_map/ppermute | solution.py:419
  45.0 7.8 %collective-permute-start.6 = (f32[4,56,128]{2,1,0:T(8,128)S(1)}, f32[4,56,128]{2,1,0:T(8,128)S(1)}, u32[]{:S(2)}, u32[]{:S(2)}) collective-permute-start(f32[4,56,128]{2,1,0:T(8,128)S(1)} %pad_maximum_fusion.1.side_ref), channel_id=1, source_target_pairs={{4,0},{5,1},{6,2},{7,3},{8,4},{9,5},{10,6},{11,7},{12,8},{13,9},{1... | collective-permute-start | bytes 344072 | tf_op jit(solution)/shard_map/ppermute | solution.py:420
  46.3 0.7 copy-start.9
  53.6 0.8 copy-start.4
  54.4 0.8 copy-start.5
  129.4 19.8 %collective-permute-start.7 = (f32[23,32,128]{2,1,0:T(8,128)}, f32[23,32,128]{2,1,0:T(8,128)S(1)}, u32[]{:S(2)}, u32[]{:S(2)}) collective-permute-start(f32[23,32,128]{2,1,0:T(8,128)} %get-tuple-element.31), channel_id=1, source_target_pairs={{0,4},{1,5},{2,6},{3,7},{4,8},{5,9},{6,10},{7,11},{8,12},{9,13},{1... | collective-permute-start | bytes 1130504 | tf_op jit(solution)/shard_map/ppermute | solution.py:419
  132.0 17.2 %collective-permute-start.8 = (f32[23,32,128]{2,1,0:T(8,128)}, f32[23,32,128]{2,1,0:T(8,128)S(1)}, u32[]{:S(2)}, u32[]{:S(2)}) collective-permute-start(f32[23,32,128]{2,1,0:T(8,128)} %get-tuple-element.32), channel_id=1, source_target_pairs={{4,0},{5,1},{6,2},{7,3},{8,4},{9,5},{10,6},{11,7},{12,8},{13,9},{1... | collective-permute-start | bytes 1130504 | tf_op jit(solution)/shard_map/ppermute | solution.py:420
  149.2 1.0 copy-start.1
  151.5 27.7 %all-to-all-start.2 = ((f32[64,1,2176]{2,1,0:T(1,128)}), f32[64,1,2176]{2,1,0:T(1,128)S(1)}, u32[]{:S(2)}, u32[]{:S(2)}) async-start(f32[64,1,2176]{2,1,0:T(1,128)} %bitcast.13), calls=%async_computation.2 | async-start | bytes 1114112 | tf_op jit(solution)/shard_map/all_to_all | solution.py:490

commit v3 on v2

--- a/solution.py
+++ b/solution.py
@@ -25,6 +25,7 @@
 EXT = (OWN + 2 * SIDE) * TILE
 BLOCKS = OWN + 2 * SIDE - 2 * REACH
 EDGE = 2 * SIDE - 1
+RUN = 4
 RF = 40
 HIGH = 48
 RB = CH * M
@@ -226,22 +227,20 @@
         at = 2 * (SIDE - REACH) + i
         rows[at * RF : (at + 1) * RF, :] = value
 
-    def products(step, p, read):
+    def products(step, begin, count, read):
+        used = HIGH if step == 0 else 2 * RF
         got = []
-        for h in range(2):
-            b = 2 * p + h + step * REACH
-            used = HIGH if step == 0 else 2 * RF
+        for h in range(count):
+            b = begin + h + step * REACH
             field = xs[step % 2, :used, tile_at(b, 2 * REACH + 1)]
             got.append(jnp.dot(field, read(b, h), preferred_element_type=F32))
         return got
 
-    def keep(step, p, got):
+    def keep(step, begin, got):
         kept = {0: 1, 1: 2, 3: 3}.get(step)
-        for h in range(2):
-            b = 2 * p + h + step * REACH
-            value = got[h][:RF]
-            if step > 0:
-                value = value + got[h][RF:]
+        for h, value in enumerate(got):
+            b = begin + h + step * REACH
+            value = value[:RF] if step == 0 else value[:RF] + value[RF:]
             if step < 3:
                 xs[(step + 1) % 2, :, tile_at(b + REACH)] = parts(value)
             if kept is not None:
@@ -249,44 +248,51 @@
                 rows[pl.ds(start, RF), :] = value[:, :LANE]
                 rows[pl.ds(start + RF, RF), :] = value[:, LANE:]
 
-    def build_pair(p, stage):
-        for h in range(2):
-            plain(2 * p + h, h, stage)
-
-    def fix_pair(p, stage):
-        for h in range(2):
-            clipped(2 * p + h, h, stage)
-
-    def use_and_build(p, stage, following):
-        got = products(0, p, lambda b, h: stage[h])
-        build_pair(p + 1, following)
-        keep(0, p, got)
-        fix_pair(p + 1, following)
-
-    build_pair(0, stage_a)
-    fix_pair(0, stage_a)
-
-    def two_pairs(i, carry):
-        use_and_build(2 * i, stage_a, stage_b)
-        use_and_build(2 * i + 1, stage_b, stage_a)
+    def build_group(begin, count, stage):
+        for h in range(count):
+            plain(begin + h, h, stage)
+
+    def fix_group(begin, count, stage):
+        for h in range(count):
+            clipped(begin + h, h, stage)
+
+    def use_and_build(begin, stage, count, following):
+        got = products(0, begin, RUN, lambda b, h: stage[h])
+        build_group(begin + RUN, count, following)
+        keep(0, begin, got)
+        fix_group(begin + RUN, count, following)
+
+    build_group(0, RUN, stage_a)
+    fix_group(0, RUN, stage_a)
+
+    def two_groups(i, carry):
+        use_and_build(2 * RUN * i, stage_a, RUN, stage_b)
+        use_and_build(2 * RUN * i + RUN, stage_b, RUN, stage_a)
         return carry
 
-    last = BLOCKS // 2 - 1
-    lax.fori_loop(0, last // 2, two_pairs, 0)
-    keep(0, last, products(0, last, lambda b, h: stage_a[h]))
+    turns = BLOCKS // (2 * RUN) - 1
+    lax.fori_loop(0, turns, two_groups, 0)
+    begin = 2 * RUN * turns
+    rest = BLOCKS - begin - 2 * RUN
+    use_and_build(begin, stage_a, RUN, stage_b)
+    use_and_build(begin + RUN, stage_b, rest, stage_a)
+    keep(0, begin + 2 * RUN, products(0, begin + 2 * RUN, rest, lambda b, h: stage_a[h]))
 
     for step in range(1, 4):
 
-        def forward(scored, p, carry):
-            got = products(step, p, lambda b, h: band[b])
-            if scored:
-                score(step - 1, p)
-            keep(step, p, got)
+        def forward(scores, count, g, carry):
+            got = products(step, RUN * g, count, lambda b, h: band[b])
+            for index in range(scores):
+                score(step - 1, g * scores + index)
+            keep(step, RUN * g, got)
             return carry
 
-        split = CH * GROUP
-        lax.fori_loop(0, split, functools.partial(forward, True), 0)
-        lax.fori_loop(split, BLOCKS // 2 - REACH * step, functools.partial(forward, False), 0)
+        size = BLOCKS - 2 * REACH * step
+        scored = OWN // RUN
+        lax.fori_loop(0, scored, functools.partial(forward, CH * GROUP // scored, RUN), 0)
+        lax.fori_loop(scored, size // RUN, functools.partial(forward, 0, RUN), 0)
+        if size % RUN:
+            forward(0, size % RUN, size // RUN, 0)
 
     def only_score(index, carry):
         score(3, index)
@@ -324,28 +330,29 @@
             lax.fori_loop(0, BLOCKS - 2 * first, refill, 0)
         total[...] = jnp.zeros_like(total)
 
-        def backward(p, carry):
+        def backward(count, g, carry):
+            begin = RUN * g + first
             got = []
-            for h in range(2):
-                b = 2 * p + h + first
-                got.append(
-                    lax.dot_general(
-                        gs[: 2 * RB, tile_at(b + REACH)],
-                        band[b],
-                        (((1,), (1,)), ((), ())),
-                        preferred_element_type=F32,
-                    )
+            for h in range(count):
+                value = lax.dot_general(
+                    gs[: 2 * RB, tile_at(begin + h + REACH)],
+                    band[begin + h],
+                    (((1,), (1,)), ((), ())),
+                    preferred_element_type=F32,
                 )
-            one, two = (value[:RB] + value[RB:] for value in got)
-            at = tile_at(2 * p + first)
-            total[:, at] = total[:, at] + one[:, :TILE]
-            at = tile_at(2 * p + first + 1, 2 * REACH)
-            total[:, at] = total[:, at] + (one[:, TILE:] + two[:, :-TILE])
-            at = tile_at(2 * p + first + 2 * REACH + 1)
-            total[:, at] = total[:, at] + two[:, -TILE:]
+                got.append(value[:RB] + value[RB:])
+            for t in range(2 * REACH + count):
+                pieces = [
+                    got[h][:, (t - h) * TILE : (t - h + 1) * TILE] for h in range(count) if 0 <= t - h <= 2 * REACH
+                ]
+                at = tile_at(begin + t)
+                total[:, at] = total[:, at] + functools.reduce(jnp.add, pieces)
             return carry
 
-        lax.fori_loop(0, (BLOCKS - 2 * first) // 2, backward, 0)
+        size = BLOCKS - 2 * first
+        lax.fori_loop(0, size // RUN, functools.partial(backward, RUN), 0)
+        if size % RUN:
+            backward(size % RUN, size // RUN, 0)
 
     for i in range(CHUNKS):
         at = 2 * SIDE + i
@@ -467,8 +474,8 @@
             pltpu.VMEM((4 * CHUNKS * RB, LANE), F32),
             pltpu.VMEM((RB, EXT), F32),
             pltpu.VMEM((4 * PER, LANE), F32),
-            pltpu.VMEM((2, BAND, TILE), BF16),
-            pltpu.VMEM((2, BAND, TILE), BF16),
+            pltpu.VMEM((RUN, BAND, TILE), BF16),
+            pltpu.VMEM((RUN, BAND, TILE), BF16),
             pltpu.VMEM((BAND, TILE), BF16),
         ],
         scalars=2,

time: 181 us -> 177 us (0.978)
  Pallas kernels: 78.2 us -> 74.1 us
    pallas_call x1, Pallas kernels: 74.2 us -> 70.1 us  [local(): call(functools.partial(main_body, cells * BLOCK), 'smooth_score_back', [s...]
where the time goes in v3:
time: 177 us; the launch traced here: 176 us
  Pallas kernels  74.1 us (42%)
  starting transfers between devices  48.6 us (27%)
  waiting for transfers between devices  28.3 us (16%)
  blocking collectives  15.9 us (9%)
  local copies, waits for them, and re-layouts  7.25 us (4%)
    pallas_call x1, Pallas kernels, local(): call(functools.partial(main_body, cells * BLOCK), 'smooth_score_back', [s...  70.1 us
    all_to_all x1, waiting for transfers between devices, local(): lax.all_to_all(packed.reshape(slots, 1, NOTE * LANE), ('member', 'cell'),...  17.9 us
    all_to_all x1, blocking collectives, local(): lax.all_to_all(sums, 'cell', 0, 0, axis_index_groups=by_column, tiled=True)  15.9 us
    all_to_all x1, starting transfers between devices, local(): lax.all_to_all(send.reshape(slots, CH * PER, LANE), ('member', 'cell'), 0...  15 us
    ppermute x3, starting transfers between devices, local(): lax.ppermute(piece, 'cell', among_four(lambda x: (x + shift) % GROUP))  10.1 us
    ppermute x3, starting transfers between devices, exchange(): lax.ppermute(to_right, 'cell', among_rows(lambda y: y + 1))  9.86 us
    all_to_all x1, starting transfers between devices, local(): lax.all_to_all(packed.reshape(slots, 1, NOTE * LANE), ('member', 'cell'),...  9.81 us
    unnamed x20, local copies, waits for them, and re-layouts  6.34 us
  transfers between devices with their start and end apart: 11, of which 5 were waited for; matrix products, arithmetic and copies ran while one was open for 1% of the time, Pallas kernels for 0%

profile of v3, /device:TPU:1, one launch (start us, length us, event | category | flops | bytes accessed | tf_op | source)
XLA Modules:
  0.0 176.1 jit_solution(15645089959539411344)
XLA Ops:
  0.6 0.9 copy-done.2
  1.6 1.0 pack.1
  2.6 15.0 %all-to-all-start = ((f32[64,16,128]{2,1,0:T(8,128)}), f32[64,16,128]{2,1,0:T(8,128)S(1)}, u32[]{:S(2)}, u32[]{:S(2)}) async-start(f32[64,16,128]{2,1,0:T(8,128)} %bitcast.2), calls=%async_computation | async-start | bytes 1048576 | tf_op jit(solution)/shard_map/all_to_all | solution.py:433
  19.2 4.8 %collective-permute-start.1 = (f32[56,128]{1,0:T(8,128)S(1)}, f32[56,128]{1,0:T(8,128)S(1)}, u32[]{:S(2)}, u32[]{:S(2)}) collective-permute-start(f32[56,128]{1,0:T(8,128)S(1)} %get-tuple-element.50), channel_id=1, source_target_pairs={{0,2},{1,3},{2,0},{3,1},{4,6},{5,7},{6,4},{7,5},{8,10},{9,11},{10,... | collective-permute-start | bytes 86024 | tf_op jit(solution)/shard_map/ppermute | solution.py:446
  24.0 2.8 %collective-permute-start.2 = (f32[56,128]{1,0:T(8,128)S(1)}, f32[56,128]{1,0:T(8,128)S(1)}, u32[]{:S(2)}, u32[]{:S(2)}) collective-permute-start(f32[56,128]{1,0:T(8,128)S(1)} %get-tuple-element.51), channel_id=1, source_target_pairs={{0,3},{1,0},{2,1},{3,2},{4,7},{5,4},{6,5},{7,6},{8,11},{9,8},{10,9... | collective-permute-start | bytes 86024 | tf_op jit(solution)/shard_map/ppermute | solution.py:446
  26.8 2.5 %collective-permute-start = (f32[56,128]{1,0:T(8,128)S(1)}, f32[56,128]{1,0:T(8,128)S(1)}, u32[]{:S(2)}, u32[]{:S(2)}) collective-permute-start(f32[56,128]{1,0:T(8,128)S(1)} %get-tuple-element.49), channel_id=1, source_target_pairs={{0,1},{1,2},{2,3},{3,0},{4,5},{5,6},{6,7},{7,4},{8,9},{9,10},{10,1... | collective-permute-start | bytes 86024 | tf_op jit(solution)/shard_map/ppermute | solution.py:446
  29.4 3.7 %collective-permute-done = f32[56,128]{1,0:T(8,128)S(1)} collective-permute-done((f32[56,128]{1,0:T(8,128)S(1)}, f32[56,128]{1,0:T(8,128)S(1)}, u32[]{:S(2)}, u32[]{:S(2)}) %collective-permute-start) | collective-permute-done | bytes 28704 | tf_op jit(solution)/shard_map/ppermute | solution.py:446
  33.1 1.7 all-to-all-done.recv_ref
  35.6 0.8 copy-done
  36.5 3.2 %collective-permute-start.3 = (f32[792,128]{1,0:T(8,128)S(1)}, f32[792,128]{1,0:T(8,128)S(1)}, u32[]{:S(2)}, u32[]{:S(2)}) collective-permute-start(f32[792,128]{1,0:T(8,128)S(1)} %get-tuple-element.27), channel_id=1, source_target_pairs={{0,4},{1,5},{2,6},{3,7},{4,8},{5,9},{6,10},{7,11},{8,12},{9,13},{1... | collective-permute-start | bytes 1216520 | tf_op jit(solution)/shard_map/ppermute | solution.py:426
  39.7 1.3 collective-permute-start.4
  41.0 4.0 %collective-permute-start.5 = (f32[4,56,128]{2,1,0:T(8,128)S(1)}, f32[4,56,128]{2,1,0:T(8,128)S(1)}, u32[]{:S(2)}, u32[]{:S(2)}) collective-permute-start(f32[4,56,128]{2,1,0:T(8,128)S(1)} %pad_maximum_fusion.1.side_ref), channel_id=1, source_target_pairs={{0,4},{1,5},{2,6},{3,7},{4,8},{5,9},{6,10},{7,11},{8,12},{9,13},{1... | collective-permute-start | bytes 344072 | tf_op jit(solution)/shard_map/ppermute | solution.py:426
  45.0 1.3 collective-permute-start.6
  47.8 1.2 collective-permute-done.5
  49.0 3.9 %collective-permute-done.6 = f32[4,56,128]{2,1,0:T(8,128)S(1)} collective-permute-done((f32[4,56,128]{2,1,0:T(8,128)S(1)}, f32[4,56,128]{2,1,0:T(8,128)S(1)}, u32[]{:S(2)}, u32[]{:S(2)}) %collective-permute-start.6) | collective-permute-done | bytes 114720 | tf_op jit(solution)/shard_map/ppermute | solution.py:427
  55.1 70.1 %smooth_score_back.1 = (f32[32,32,128]{2,1,0:T(8,128)}, f32[23,32,128]{2,1,0:T(8,128)}, f32[23,32,128]{2,1,0:T(8,128)}, f32[8,8,128]{2,1,0:T(8,128)}) custom-call(s32[2]{0:T(128)} %copy-done.3, f32[2]{0:T(128)} %fusion.1.weight_ref, f32[32,40,128]{2,1,0:T(8,128)} %copy-done, f32[792,128]{1,0:T(8,128)} %copy-done.4, f32[792,128]{1,0:T(8,128)} %copy-done.5, ...), custom_call_target="tpu_custom_call" | custom-call | tf_op jit(solution)/shard_map/smooth_score_back/pallas_call | solution.py:466
  125.2 2.7 %collective-permute-start.7 = (f32[23,32,128]{2,1,0:T(8,128)}, f32[23,32,128]{2,1,0:T(8,128)S(1)}, u32[]{:S(2)}, u32[]{:S(2)}) collective-permute-start(f32[23,32,128]{2,1,0:T(8,128)} %get-tuple-element.31), channel_id=1, source_target_pairs={{0,4},{1,5},{2,6},{3,7},{4,8},{5,9},{6,10},{7,11},{8,12},{9,13},{1... | collective-permute-start | bytes 1130504 | tf_op jit(solution)/shard_map/ppermute | solution.py:426
  127.9 1.3 collective-permute-start.8
  129.2 15.9 %all_to_all.15.sums_ref = f32[8,8,128]{2,1,0:T(8,128)S(1)} all-to-all(f32[8,8,128]{2,1,0:T(8,128)} %get-tuple-element.33), channel_id=1, replica_groups={{0,4,8,12,16,20,24,28},{1,5,9,13,17,21,25,29},{2,6,10,14,18,22,26,30},{..., dimensions={0} | all-to-all | bytes 65536 | tf_op jit(solution)/shard_map/all_to_all | solution.py:488
  145.1 1.0 copy-done.1
  146.1 1.3 gather_grad.1
  147.4 9.8 %all-to-all-start.2 = ((f32[64,1,2176]{2,1,0:T(1,128)}), f32[64,1,2176]{2,1,0:T(1,128)S(1)}, u32[]{:S(2)}, u32[]{:S(2)}) async-start(f32[64,1,2176]{2,1,0:T(1,128)} %bitcast.13), calls=%async_computation.2 | async-start | bytes 1114112 | tf_op jit(solution)/shard_map/all_to_all | solution.py:497
  157.2 17.9 %all-to-all-done.2 = f32[64,1,2176]{2,1,0:T(1,128)S(1)} async-done(((f32[64,1,2176]{2,1,0:T(1,128)}), f32[64,1,2176]{2,1,0:T(1,128)S(1)}, u32[]{:S(2)}, u32[]{:S(2)}) %all-to-all-start.2) | async-done | bytes 557088 | tf_op jit(solution)/shard_map/all_to_all | solution.py:497
  175.1 0.9 spread.1
  (38 shorter events, 6.2 us)
Async XLA Ops:
  0.6 0.9 copy-start.2
  2.6 15.0 %copy-start.6 = (bf16[100,1024]{1,0:T(8,128)(2,1)S(1)}, bf16[100,1024]{1,0:T(8,128)(2,1)}, u32[]{:S(2)}) copy-start(bf16[100,1024]{1,0:T(8,128)(2,1)} %param.6) | copy-start | bytes 614404
  2.6 32.2 %all-to-all-start = ((f32[64,16,128]{2,1,0:T(8,128)}), f32[64,16,128]{2,1,0:T(8,128)S(1)}, u32[]{:S(2)}, u32[]{:S(2)}) async-start(f32[64,16,128]{2,1,0:T(8,128)} %bitcast.2), calls=%async_computation | async-start | bytes 1048576 | tf_op jit(solution)/shard_map/all_to_all | solution.py:433
  17.7 0.7 copy-start.7
  18.5 0.7 copy-start.8
  19.2 10.2 %collective-permute-start.1 = (f32[56,128]{1,0:T(8,128)S(1)}, f32[56,128]{1,0:T(8,128)S(1)}, u32[]{:S(2)}, u32[]{:S(2)}) collective-permute-start(f32[56,128]{1,0:T(8,128)S(1)} %get-tuple-element.50), channel_id=1, source_target_pairs={{0,2},{1,3},{2,0},{3,1},{4,6},{5,7},{6,4},{7,5},{8,10},{9,11},{10,... | collective-permute-start | bytes 86024 | tf_op jit(solution)/shard_map/ppermute | solution.py:446
  24.0 5.4 %collective-permute-start.2 = (f32[56,128]{1,0:T(8,128)S(1)}, f32[56,128]{1,0:T(8,128)S(1)}, u32[]{:S(2)}, u32[]{:S(2)}) collective-permute-start(f32[56,128]{1,0:T(8,128)S(1)} %get-tuple-element.51), channel_id=1, source_target_pairs={{0,3},{1,0},{2,1},{3,2},{4,7},{5,4},{6,5},{7,6},{8,11},{9,8},{10,9... | collective-permute-start | bytes 86024 | tf_op jit(solution)/shard_map/ppermute | solution.py:446
  26.8 6.3 %collective-permute-start = (f32[56,128]{1,0:T(8,128)S(1)}, f32[56,128]{1,0:T(8,128)S(1)}, u32[]{:S(2)}, u32[]{:S(2)}) collective-permute-start(f32[56,128]{1,0:T(8,128)S(1)} %get-tuple-element.49), channel_id=1, source_target_pairs={{0,1},{1,2},{2,3},{3,0},{4,5},{5,6},{6,7},{7,4},{8,9},{9,10},{10,1... | collective-permute-start | bytes 86024 | tf_op jit(solution)/shard_map/ppermute | solution.py:446
  29.4 5.4 %copy-start.3 = (s32[2]{0:T(128)}, s32[2]{0:T(128)S(1)}, u32[]{:S(2)}) copy-start(s32[2]{0:T(128)S(1)} %pad_add_fusion.place_ref) | copy-start | bytes 28
  35.6 0.9 copy-start
  36.5 17.1 %collective-permute-start.3 = (f32[792,128]{1,0:T(8,128)S(1)}, f32[792,128]{1,0:T(8,128)S(1)}, u32[]{:S(2)}, u32[]{:S(2)}) collective-permute-start(f32[792,128]{1,0:T(8,128)S(1)} %get-tuple-element.27), channel_id=1, source_target_pairs={{0,4},{1,5},{2,6},{3,7},{4,8},{5,9},{6,10},{7,11},{8,12},{9,13},{1... | collective-permute-start | bytes 1216520 | tf_op jit(solution)/shard_map/ppermute | solution.py:426
  39.7 13.9 %collective-permute-start.4 = (f32[792,128]{1,0:T(8,128)S(1)}, f32[792,128]{1,0:T(8,128)S(1)}, u32[]{:S(2)}, u32[]{:S(2)}) collective-permute-start(f32[792,128]{1,0:T(8,128)S(1)} %get-tuple-element.28), channel_id=1, source_target_pairs={{4,0},{5,1},{6,2},{7,3},{8,4},{9,5},{10,6},{11,7},{12,8},{13,9},{1... | collective-permute-start | bytes 1216520 | tf_op jit(solution)/shard_map/ppermute | solution.py:427
  41.0 8.0 %collective-permute-start.5 = (f32[4,56,128]{2,1,0:T(8,128)S(1)}, f32[4,56,128]{2,1,0:T(8,128)S(1)}, u32[]{:S(2)}, u32[]{:S(2)}) collective-permute-start(f32[4,56,128]{2,1,0:T(8,128)S(1)} %pad_maximum_fusion.1.side_ref), channel_id=1, source_target_pairs={{0,4},{1,5},{2,6},{3,7},{4,8},{5,9},{6,10},{7,11},{8,12},{9,13},{1... | collective-permute-start | bytes 344072 | tf_op jit(solution)/shard_map/ppermute | solution.py:426
  45.0 7.8 %collective-permute-start.6 = (f32[4,56,128]{2,1,0:T(8,128)S(1)}, f32[4,56,128]{2,1,0:T(8,128)S(1)}, u32[]{:S(2)}, u32[]{:S(2)}) collective-permute-start(f32[4,56,128]{2,1,0:T(8,128)S(1)} %pad_maximum_fusion.1.side_ref), channel_id=1, source_target_pairs={{4,0},{5,1},{6,2},{7,3},{8,4},{9,5},{10,6},{11,7},{12,8},{13,9},{1... | collective-permute-start | bytes 344072 | tf_op jit(solution)/shard_map/ppermute | solution.py:427
  46.3 0.7 copy-start.9
  53.6 0.8 copy-start.4
  54.4 0.8 copy-start.5
  125.2 19.8 %collective-permute-start.7 = (f32[23,32,128]{2,1,0:T(8,128)}, f32[23,32,128]{2,1,0:T(8,128)S(1)}, u32[]{:S(2)}, u32[]{:S(2)}) collective-permute-start(f32[23,32,128]{2,1,0:T(8,128)} %get-tuple-element.31), channel_id=1, source_target_pairs={{0,4},{1,5},{2,6},{3,7},{4,8},{5,9},{6,10},{7,11},{8,12},{9,13},{1... | collective-permute-start | bytes 1130504 | tf_op jit(solution)/shard_map/ppermute | solution.py:426
  127.9 17.2 %collective-permute-start.8 = (f32[23,32,128]{2,1,0:T(8,128)}, f32[23,32,128]{2,1,0:T(8,128)S(1)}, u32[]{:S(2)}, u32[]{:S(2)}) collective-permute-start(f32[23,32,128]{2,1,0:T(8,128)} %get-tuple-element.32), channel_id=1, source_target_pairs={{4,0},{5,1},{6,2},{7,3},{8,4},{9,5},{10,6},{11,7},{12,8},{13,9},{1... | collective-permute-start | bytes 1130504 | tf_op jit(solution)/shard_map/ppermute | solution.py:427
  145.1 1.0 copy-start.1
  147.4 27.7 %all-to-all-start.2 = ((f32[64,1,2176]{2,1,0:T(1,128)}), f32[64,1,2176]{2,1,0:T(1,128)S(1)}, u32[]{:S(2)}, u32[]{:S(2)}) async-start(f32[64,1,2176]{2,1,0:T(1,128)} %bitcast.13), calls=%async_computation.2 | async-start | bytes 1114112 | tf_op jit(solution)/shard_map/all_to_all | solution.py:497

commit v4 on v3

--- a/solution.py
+++ b/solution.py
@@ -26,9 +26,11 @@
 BLOCKS = OWN + 2 * SIDE - 2 * REACH
 EDGE = 2 * SIDE - 1
 RUN = 4
+FIRST = 2
 RF = 40
 HIGH = 48
 RB = CH * M
+SPARE = 4 * CHUNKS * RF
 RT = RB + CH
 WIRE = -(-(EDGE * RT + RF - RT) // 8) * 8
 AUX = (CH + NEIGH + 1) * PER
@@ -123,7 +125,7 @@
             chunk = CHUNKS - 2 * SIDE + 2 * (b + REACH) + h
             x = (chunk % CHUNKS) // PER
             piece = (chunk // CHUNKS) * GROUP + shift_of(x, mine)
-            halves.append(aux_ref[piece, pl.ds((CH + k) * PER + chunk % PER, 1), :])
+            halves.append(aux_ref[piece, pl.ds(k * PER + chunk % PER, 1), :])
         return jnp.concatenate(halves, axis=1) - (first_cell + b * TILE).astype(F32)
 
     def plain(b, h, stage):
@@ -164,17 +166,17 @@
     return plain, clipped
 
 
-def scorer(weight_ref, mine, aux_ref, rows, slopes, sums):
+def scorer(weight_ref, mine, side_ref, rows, slopes, sums):
     square = DELTA * DELTA
     sums[...] = jnp.zeros_like(sums)
 
     def one(level, index):
         c = index // GROUP
         x = index % GROUP
-        base = level * (2 * BLOCKS * RF) + (2 * (SIDE - REACH) + x * PER) * RF
+        base = (level * CHUNKS + x * PER) * RF
         fields = [rows[pl.ds(base + c * M + m, PER, stride=RF), :] for m in range(M)]
         truth = rows[pl.ds(base + RB + c, PER, stride=RF), :]
-        coef = aux_ref[GROUP + shift_of(x, mine), AREA_AT:, :] * weight_ref[c]
+        coef = side_ref[shift_of(x, mine), AREA_AT:, :] * weight_ref[c]
         slope = [None] * M
         inverse = jnp.zeros((PER, LANE), F32)
         for a in range(M):
@@ -205,13 +207,13 @@
 
 
 def main_body(
-    cells, place_ref, weight_ref, own_ref, left_ref, right_ref, aux_ref,
+    cells, place_ref, weight_ref, own_ref, left_ref, right_ref, side_ref, aux_ref,
     center_ref, outl_ref, outr_ref, loss_ref, band, xs, rows, slopes, total, sums, stage_a, stage_b, pattern,
 ):
     row_group = place_ref[0]
     mine = place_ref[1]
     plain, clipped = builder(row_group, mine, aux_ref, band, pattern, cells)
-    score = scorer(weight_ref, mine, aux_ref, rows, slopes, sums)
+    score = scorer(weight_ref, mine, side_ref, rows, slopes, sums)
 
     xs[0, :, :LANE] = jnp.zeros((2 * RF, LANE), BF16)
     xs[0, :, EXT - LANE :] = jnp.zeros((2 * RF, LANE), BF16)
@@ -224,8 +226,7 @@
         value = own_ref[i]
         at = 2 * SIDE + i
         xs[0, :, at * LANE : (at + 1) * LANE] = parts(value)
-        at = 2 * (SIDE - REACH) + i
-        rows[at * RF : (at + 1) * RF, :] = value
+        rows[i * RF : (i + 1) * RF, :] = value
 
     def products(step, begin, count, read):
         used = HIGH if step == 0 else 2 * RF
@@ -244,7 +245,10 @@
             if step < 3:
                 xs[(step + 1) % 2, :, tile_at(b + REACH)] = parts(value)
             if kept is not None:
-                start = pl.multiple_of(kept * (2 * BLOCKS * RF) + b * (2 * RF), RF)
+                place = b - (SIDE - REACH)
+                mine = (place >= 0) & (place < OWN)
+                start = jnp.where(mine, kept * (CHUNKS * RF) + place * (2 * RF), SPARE)
+                start = pl.multiple_of(start, RF)
                 rows[pl.ds(start, RF), :] = value[:, :LANE]
                 rows[pl.ds(start + RF, RF), :] = value[:, LANE:]
 
@@ -257,26 +261,26 @@
             clipped(begin + h, h, stage)
 
     def use_and_build(begin, stage, count, following):
-        got = products(0, begin, RUN, lambda b, h: stage[h])
-        build_group(begin + RUN, count, following)
+        got = products(0, begin, FIRST, lambda b, h: stage[h])
+        build_group(begin + FIRST, count, following)
         keep(0, begin, got)
-        fix_group(begin + RUN, count, following)
-
-    build_group(0, RUN, stage_a)
-    fix_group(0, RUN, stage_a)
+        fix_group(begin + FIRST, count, following)
+
+    build_group(0, FIRST, stage_a)
+    fix_group(0, FIRST, stage_a)
 
     def two_groups(i, carry):
-        use_and_build(2 * RUN * i, stage_a, RUN, stage_b)
-        use_and_build(2 * RUN * i + RUN, stage_b, RUN, stage_a)
+        use_and_build(2 * FIRST * i, stage_a, FIRST, stage_b)
+        use_and_build(2 * FIRST * i + FIRST, stage_b, FIRST, stage_a)
         return carry
 
-    turns = BLOCKS // (2 * RUN) - 1
+    turns = BLOCKS // (2 * FIRST) - 1
     lax.fori_loop(0, turns, two_groups, 0)
-    begin = 2 * RUN * turns
-    rest = BLOCKS - begin - 2 * RUN
-    use_and_build(begin, stage_a, RUN, stage_b)
-    use_and_build(begin + RUN, stage_b, rest, stage_a)
-    keep(0, begin + 2 * RUN, products(0, begin + 2 * RUN, rest, lambda b, h: stage_a[h]))
+    begin = 2 * FIRST * turns
+    rest = BLOCKS - begin - 2 * FIRST
+    use_and_build(begin, stage_a, FIRST, stage_b)
+    use_and_build(begin + FIRST, stage_b, rest, stage_a)
+    keep(0, begin + 2 * FIRST, products(0, begin + 2 * FIRST, rest, lambda b, h: stage_a[h]))
 
     for step in range(1, 4):
 
@@ -300,7 +304,7 @@
 
     lax.fori_loop(0, CH * GROUP, only_score, 0)
     partial = [jnp.sum(sums[level * PER : (level + 1) * PER, :], axis=0, keepdims=True) for level in range(4)]
-    partial.append(jnp.sum(aux_ref[GROUP, AREA_AT:, :], axis=0, keepdims=True) * (1.0 / M))
+    partial.append(jnp.sum(side_ref[0, AREA_AT:, :], axis=0, keepdims=True) * (1.0 / M))
     partial.append(jnp.zeros((PER - len(partial), LANE), F32))
     partial = jnp.concatenate(partial, axis=0)
     for i in range(loss_ref.shape[0]):
@@ -460,8 +464,9 @@
     )(place, recv, side)
     own, side, to_left, to_right = lax.optimization_barrier((own, side, to_left, to_right))
     left, right = exchange(to_left, to_right)
-    before, after = exchange(side, side)
-    aux = jnp.concatenate([before, side, after])
+    index = side[:, CH * PER : AREA_AT, :]
+    before, after = exchange(index, index)
+    aux = jnp.concatenate([before, index, after])
 
     center, out_left, out_right, sums = call(
         functools.partial(main_body, cells * BLOCK),
@@ -470,18 +475,18 @@
         [
             pltpu.VMEM((BLOCKS, BAND, TILE), BF16),
             pltpu.VMEM((2, 2 * RF, EXT), BF16),
-            pltpu.VMEM((4 * 2 * BLOCKS * RF, LANE), F32),
+            pltpu.VMEM((SPARE + 2 * RF, LANE), F32),
             pltpu.VMEM((4 * CHUNKS * RB, LANE), F32),
             pltpu.VMEM((RB, EXT), F32),
             pltpu.VMEM((4 * PER, LANE), F32),
-            pltpu.VMEM((RUN, BAND, TILE), BF16),
-            pltpu.VMEM((RUN, BAND, TILE), BF16),
+            pltpu.VMEM((FIRST, BAND, TILE), BF16),
+            pltpu.VMEM((FIRST, BAND, TILE), BF16),
             pltpu.VMEM((BAND, TILE), BF16),
         ],
         scalars=2,
-        vectors=4,
-        limit=58,
-    )(place, weights, own, left, right, aux)
+        vectors=5,
+        limit=48,
+    )(place, weights, own, left, right, side, aux)
 
     arrived = exchange(out_left, out_right)
     by_column = [[y * GROUP + x for y in rows] for x in range(GROUP)]

time: 177 us -> 170 us (0.960)
  local copies, waits for them, and re-layouts: 7.25 us -> 3.35 us
    unnamed x20 -> x10, local copies, waits for them, and re-layouts: 6.34 us -> 2.94 us
  transfers between devices with their start and end apart: 11 -> 11, of which waited for: 5 -> 5; matrix products, arithmetic and copies ran while one was open for 1% -> 0% of each run, Pallas kernels for 0% -> 0%
where the time goes in v4:
time: 170 us
  Pallas kernels  72.8 us (43%)
  starting transfers between devices  48.8 us (29%)
  waiting for transfers between devices  27.8 us (16%)
  blocking collectives  15.7 us (9%)
  local copies, waits for them, and re-layouts  3.35 us (2%)
    pallas_call x1, Pallas kernels, local(): call(functools.partial(main_body, cells * BLOCK), 'smooth_score_back', [s...  68.8 us
    all_to_all x1, waiting for transfers between devices, local(): lax.all_to_all(packed.reshape(slots, 1, NOTE * LANE), ('member', 'cell'),...  17.9 us
    all_to_all x1, blocking collectives, local(): lax.all_to_all(sums, 'cell', 0, 0, axis_index_groups=by_column, tiled=True)  15.7 us
    all_to_all x1, starting transfers between devices, local(): lax.all_to_all(send.reshape(slots, CH * PER, LANE), ('member', 'cell'), 0...  15 us
    ppermute x3, starting transfers between devices, local(): lax.ppermute(piece, 'cell', among_four(lambda x: (x + shift) % GROUP))  10.1 us
    all_to_all x1, starting transfers between devices, local(): lax.all_to_all(packed.reshape(slots, 1, NOTE * LANE), ('member', 'cell'),...  9.94 us
    ppermute x3, starting transfers between devices, exchange(): lax.ppermute(to_right, 'cell', among_rows(lambda y: y + 1))  9.89 us
    ppermute x3, starting transfers between devices, exchange(): lax.ppermute(to_left, 'cell', among_rows(lambda y: y - 1))  3.88 us
  transfers between devices with their start and end apart: 11, of which 5 were waited for; matrix products, arithmetic and copies ran while one was open for 0% of the time, Pallas kernels for 0%

profile of v4, /device:TPU:1, one launch (start us, length us, event | category | flops | bytes accessed | tf_op | source)
XLA Modules:
  0.0 169.6 jit_solution(15557195821248211461)
XLA Ops:
  0.6 0.9 copy-done
  1.6 1.0 pack.1
  2.6 15.0 %all-to-all-start = ((f32[64,16,128]{2,1,0:T(8,128)}), f32[64,16,128]{2,1,0:T(8,128)S(1)}, u32[]{:S(2)}, u32[]{:S(2)}) async-start(f32[64,16,128]{2,1,0:T(8,128)} %bitcast.2), calls=%async_computation | async-start | bytes 1048576 | tf_op jit(solution)/shard_map/all_to_all | solution.py:437
  18.5 0.7 copy-done.3
  19.2 4.8 %collective-permute-start.1 = (f32[56,128]{1,0:T(8,128)S(1)}, f32[56,128]{1,0:T(8,128)S(1)}, u32[]{:S(2)}, u32[]{:S(2)}) collective-permute-start(f32[56,128]{1,0:T(8,128)S(1)} %get-tuple-element.50), channel_id=1, source_target_pairs={{0,2},{1,3},{2,0},{3,1},{4,6},{5,7},{6,4},{7,5},{8,10},{9,11},{10,... | collective-permute-start | bytes 86024 | tf_op jit(solution)/shard_map/ppermute | solution.py:450
  24.0 2.8 %collective-permute-start.2 = (f32[56,128]{1,0:T(8,128)S(1)}, f32[56,128]{1,0:T(8,128)S(1)}, u32[]{:S(2)}, u32[]{:S(2)}) collective-permute-start(f32[56,128]{1,0:T(8,128)S(1)} %get-tuple-element.51), channel_id=1, source_target_pairs={{0,3},{1,0},{2,1},{3,2},{4,7},{5,4},{6,5},{7,6},{8,11},{9,8},{10,9... | collective-permute-start | bytes 86024 | tf_op jit(solution)/shard_map/ppermute | solution.py:450
  26.8 2.5 %collective-permute-start = (f32[56,128]{1,0:T(8,128)S(1)}, f32[56,128]{1,0:T(8,128)S(1)}, u32[]{:S(2)}, u32[]{:S(2)}) collective-permute-start(f32[56,128]{1,0:T(8,128)S(1)} %get-tuple-element.49), channel_id=1, source_target_pairs={{0,1},{1,2},{2,3},{3,0},{4,5},{5,6},{6,7},{7,4},{8,9},{9,10},{10,1... | collective-permute-start | bytes 86024 | tf_op jit(solution)/shard_map/ppermute | solution.py:450
  29.4 3.7 %collective-permute-done = f32[56,128]{1,0:T(8,128)S(1)} collective-permute-done((f32[56,128]{1,0:T(8,128)S(1)}, f32[56,128]{1,0:T(8,128)S(1)}, u32[]{:S(2)}, u32[]{:S(2)}) %collective-permute-start) | collective-permute-done | bytes 28704 | tf_op jit(solution)/shard_map/ppermute | solution.py:450
  33.1 1.7 all-to-all-done.recv_ref
  34.8 0.8 unpack.1
  35.6 3.2 %collective-permute-start.3 = (f32[792,128]{1,0:T(8,128)S(1)}, f32[792,128]{1,0:T(8,128)S(1)}, u32[]{:S(2)}, u32[]{:S(2)}) collective-permute-start(f32[792,128]{1,0:T(8,128)S(1)} %get-tuple-element.27), channel_id=1, source_target_pairs={{0,4},{1,5},{2,6},{3,7},{4,8},{5,9},{6,10},{7,11},{8,12},{9,13},{1... | collective-permute-start | bytes 1216520 | tf_op jit(solution)/shard_map/ppermute | solution.py:430
  38.9 1.3 collective-permute-start.4
  40.2 4.0 %collective-permute-start.5 = (f32[4,32,128]{2,1,0:T(8,128)S(1)}, f32[4,32,128]{2,1,0:T(8,128)S(1)}, u32[]{:S(2)}, u32[]{:S(2)}) collective-permute-start(f32[4,32,128]{2,1,0:T(8,128)S(1)} %slice.3), channel_id=1, source_target_pairs={{0,4},{1,5},{2,6},{3,7},{4,8},{5,9},{6,10},{7,11},{8,12},{9,13},{1... | collective-permute-start | bytes 196616 | tf_op jit(solution)/shard_map/ppermute | solution.py:430
  44.2 1.3 collective-permute-start.6
  46.4 0.7 collective-permute-done.5
  47.1 3.9 %collective-permute-done.6 = f32[4,32,128]{2,1,0:T(8,128)S(1)} collective-permute-done((f32[4,32,128]{2,1,0:T(8,128)S(1)}, f32[4,32,128]{2,1,0:T(8,128)S(1)}, u32[]{:S(2)}, u32[]{:S(2)}) %collective-permute-start.6) | collective-permute-done | bytes 65568 | tf_op jit(solution)/shard_map/ppermute | solution.py:431
  51.0 68.8 %smooth_score_back.1 = (f32[32,32,128]{2,1,0:T(8,128)S(1)}, f32[23,32,128]{2,1,0:T(8,128)S(1)}, f32[23,32,128]{2,1,0:T(8,128)S(1)}, f32[8,8,128]{2,1,0:T(8,128)S(1)}) custom-call(s32[2]{0:T(128)S(1)} %pad_add_fusion.place_ref, f32[2]{0:T(128)S(1)} %fusion.1.weight_ref, f32[32,40,128]{2,1,0:T(8,128)S(1)} %get-tuple-element.26.own_ref, ...), custom_call_target="tpu_custom_call" | custom-call | tf_op jit(solution)/shard_map/smooth_score_back/pallas_call | solution.py:471
  119.8 2.7 %collective-permute-start.7 = (f32[23,32,128]{2,1,0:T(8,128)S(1)}, f32[23,32,128]{2,1,0:T(8,128)S(1)}, u32[]{:S(2)}, u32[]{:S(2)}) collective-permute-start(f32[23,32,128]{2,1,0:T(8,128)S(1)} %get-tuple-element.31), channel_id=1, source_target_pairs={{0,4},{1,5},{2,6},{3,7},{4,8},{5,9},{6,10},{7,11},{8,12},{9,13},{1... | collective-permute-start | bytes 1130504 | tf_op jit(solution)/shard_map/ppermute | solution.py:430
  122.5 1.3 collective-permute-start.8
  123.8 15.7 %all_to_all.15.sums_ref = f32[8,8,128]{2,1,0:T(8,128)S(1)} all-to-all(f32[8,8,128]{2,1,0:T(8,128)S(1)} %get-tuple-element.33), channel_id=1, replica_groups={{0,4,8,12,16,20,24,28},{1,5,9,13,17,21,25,29},{2,6,10,14,18,22,26,30},{..., dimensions={0} | all-to-all | bytes 65536 | tf_op jit(solution)/shard_map/all_to_all | solution.py:493
  139.5 1.3 gather_grad.1
  140.7 9.9 %all-to-all-start.2 = ((f32[64,1,2176]{2,1,0:T(1,128)}), f32[64,1,2176]{2,1,0:T(1,128)S(1)}, u32[]{:S(2)}, u32[]{:S(2)}) async-start(f32[64,1,2176]{2,1,0:T(1,128)} %bitcast.13), calls=%async_computation.2 | async-start | bytes 1114112 | tf_op jit(solution)/shard_map/all_to_all | solution.py:502
  150.7 17.9 %all-to-all-done.2 = f32[64,1,2176]{2,1,0:T(1,128)S(1)} async-done(((f32[64,1,2176]{2,1,0:T(1,128)}), f32[64,1,2176]{2,1,0:T(1,128)S(1)}, u32[]{:S(2)}, u32[]{:S(2)}) %all-to-all-start.2) | async-done | bytes 557088 | tf_op jit(solution)/shard_map/all_to_all | solution.py:502
  168.6 0.9 spread.1
  (29 shorter events, 1.9 us)
Async XLA Ops:
  0.6 0.9 copy-start
  2.6 15.0 %copy-start.1 = (bf16[100,1024]{1,0:T(8,128)(2,1)S(1)}, bf16[100,1024]{1,0:T(8,128)(2,1)}, u32[]{:S(2)}) copy-start(bf16[100,1024]{1,0:T(8,128)(2,1)} %param.6) | copy-start | bytes 614404
  2.6 32.2 %all-to-all-start = ((f32[64,16,128]{2,1,0:T(8,128)}), f32[64,16,128]{2,1,0:T(8,128)S(1)}, u32[]{:S(2)}, u32[]{:S(2)}) async-start(f32[64,16,128]{2,1,0:T(8,128)} %bitcast.2), calls=%async_computation | async-start | bytes 1048576 | tf_op jit(solution)/shard_map/all_to_all | solution.py:437
  17.7 0.7 copy-start.2
  18.5 0.7 copy-start.3
  19.2 10.2 %collective-permute-start.1 = (f32[56,128]{1,0:T(8,128)S(1)}, f32[56,128]{1,0:T(8,128)S(1)}, u32[]{:S(2)}, u32[]{:S(2)}) collective-permute-start(f32[56,128]{1,0:T(8,128)S(1)} %get-tuple-element.50), channel_id=1, source_target_pairs={{0,2},{1,3},{2,0},{3,1},{4,6},{5,7},{6,4},{7,5},{8,10},{9,11},{10,... | collective-permute-start | bytes 86024 | tf_op jit(solution)/shard_map/ppermute | solution.py:450
  24.0 5.4 %collective-permute-start.2 = (f32[56,128]{1,0:T(8,128)S(1)}, f32[56,128]{1,0:T(8,128)S(1)}, u32[]{:S(2)}, u32[]{:S(2)}) collective-permute-start(f32[56,128]{1,0:T(8,128)S(1)} %get-tuple-element.51), channel_id=1, source_target_pairs={{0,3},{1,0},{2,1},{3,2},{4,7},{5,4},{6,5},{7,6},{8,11},{9,8},{10,9... | collective-permute-start | bytes 86024 | tf_op jit(solution)/shard_map/ppermute | solution.py:450
  26.8 6.3 %collective-permute-start = (f32[56,128]{1,0:T(8,128)S(1)}, f32[56,128]{1,0:T(8,128)S(1)}, u32[]{:S(2)}, u32[]{:S(2)}) collective-permute-start(f32[56,128]{1,0:T(8,128)S(1)} %get-tuple-element.49), channel_id=1, source_target_pairs={{0,1},{1,2},{2,3},{3,0},{4,5},{5,6},{6,7},{7,4},{8,9},{9,10},{10,1... | collective-permute-start | bytes 86024 | tf_op jit(solution)/shard_map/ppermute | solution.py:450
  35.6 15.3 %collective-permute-start.3 = (f32[792,128]{1,0:T(8,128)S(1)}, f32[792,128]{1,0:T(8,128)S(1)}, u32[]{:S(2)}, u32[]{:S(2)}) collective-permute-start(f32[792,128]{1,0:T(8,128)S(1)} %get-tuple-element.27), channel_id=1, source_target_pairs={{0,4},{1,5},{2,6},{3,7},{4,8},{5,9},{6,10},{7,11},{8,12},{9,13},{1... | collective-permute-start | bytes 1216520 | tf_op jit(solution)/shard_map/ppermute | solution.py:430
  38.9 12.1 %collective-permute-start.4 = (f32[792,128]{1,0:T(8,128)S(1)}, f32[792,128]{1,0:T(8,128)S(1)}, u32[]{:S(2)}, u32[]{:S(2)}) collective-permute-start(f32[792,128]{1,0:T(8,128)S(1)} %get-tuple-element.28), channel_id=1, source_target_pairs={{4,0},{5,1},{6,2},{7,3},{8,4},{9,5},{10,6},{11,7},{12,8},{13,9},{1... | collective-permute-start | bytes 1216520 | tf_op jit(solution)/shard_map/ppermute | solution.py:431
  40.2 6.9 %collective-permute-start.5 = (f32[4,32,128]{2,1,0:T(8,128)S(1)}, f32[4,32,128]{2,1,0:T(8,128)S(1)}, u32[]{:S(2)}, u32[]{:S(2)}) collective-permute-start(f32[4,32,128]{2,1,0:T(8,128)S(1)} %slice.3), channel_id=1, source_target_pairs={{0,4},{1,5},{2,6},{3,7},{4,8},{5,9},{6,10},{7,11},{8,12},{9,13},{1... | collective-permute-start | bytes 196616 | tf_op jit(solution)/shard_map/ppermute | solution.py:430
  44.2 6.8 %collective-permute-start.6 = (f32[4,32,128]{2,1,0:T(8,128)S(1)}, f32[4,32,128]{2,1,0:T(8,128)S(1)}, u32[]{:S(2)}, u32[]{:S(2)}) collective-permute-start(f32[4,32,128]{2,1,0:T(8,128)S(1)} %slice.3), channel_id=1, source_target_pairs={{4,0},{5,1},{6,2},{7,3},{8,4},{9,5},{10,6},{11,7},{12,8},{13,9},{1... | collective-permute-start | bytes 196616 | tf_op jit(solution)/shard_map/ppermute | solution.py:431
  45.5 0.7 copy-start.4
  119.8 19.7 %collective-permute-start.7 = (f32[23,32,128]{2,1,0:T(8,128)S(1)}, f32[23,32,128]{2,1,0:T(8,128)S(1)}, u32[]{:S(2)}, u32[]{:S(2)}) collective-permute-start(f32[23,32,128]{2,1,0:T(8,128)S(1)} %get-tuple-element.31), channel_id=1, source_target_pairs={{0,4},{1,5},{2,6},{3,7},{4,8},{5,9},{6,10},{7,11},{8,12},{9,13},{1... | collective-permute-start | bytes 1130504 | tf_op jit(solution)/shard_map/ppermute | solution.py:430
  122.5 17.0 %collective-permute-start.8 = (f32[23,32,128]{2,1,0:T(8,128)S(1)}, f32[23,32,128]{2,1,0:T(8,128)S(1)}, u32[]{:S(2)}, u32[]{:S(2)}) collective-permute-start(f32[23,32,128]{2,1,0:T(8,128)S(1)} %get-tuple-element.32), channel_id=1, source_target_pairs={{4,0},{5,1},{6,2},{7,3},{8,4},{9,5},{10,6},{11,7},{12,8},{13,9},{1... | collective-permute-start | bytes 1130504 | tf_op jit(solution)/shard_map/ppermute | solution.py:431
  140.7 27.8 %all-to-all-start.2 = ((f32[64,1,2176]{2,1,0:T(1,128)}), f32[64,1,2176]{2,1,0:T(1,128)S(1)}, u32[]{:S(2)}, u32[]{:S(2)}) async-start(f32[64,1,2176]{2,1,0:T(1,128)} %bitcast.13), calls=%async_computation.2 | async-start | bytes 1114112 | tf_op jit(solution)/shard_map/all_to_all | solution.py:502
